TPU v7x, 256 devices: a whole 4x4x8 slice. The times are simulated.
256 devices in a mesh: outer: 4 (over z_hi), dev: 64 (over x, z_lo, y, core).
Axes of the slice: x: 4, y: 4, z: 8 (z_hi: 4, z_lo: 2; z = z_hi * 2 + z_lo), core: 2. Of those that a mesh axis runs over, the one named last changes fastest.
Arguments:
- hidden_rows: bfloat16 [65536, 768], P(('outer', 'dev')), may hold values from -6 to 6
- out_grad: bfloat16 [65536, 4096], P(('outer', 'dev')), may hold values from -6 to 6
- expert_weights: bfloat16 [64, 768, 4096], P(None, 'dev', 'outer'), may hold values from -0.21875 to 0.21875
- need_lists: int32 [256, 2], replicated, may hold values from 0 to 63, all different within a row; in each aligned block of 256 rows (0 to 255, 256 to 511, ...) at most 32 rows name the same one
- block_pick: int32 [512], P(('outer', 'dev')), may hold values from 0 to 1
- owner_slot: int32 [64], replicated, may hold values from 0 to 63, each once
Outputs:
- layer_out: bfloat16 [65536, 4096], P(('outer', 'dev'))
- hidden_grad: bfloat16 [65536, 768], P(('outer', 'dev'))
- weight_grad: bfloat16 [64, 768, 4096], P(None, 'dev', 'outer')
Inputs may be any that keep to these rules, and one draw needn't show every extreme that they name: `need_lists`: each row names 2 different experts; every expert is named by some row, none by more than 32 rows, a bound that some block reaches.
All inputs are finite; a program needn't handle non-finite values.
Results may differ from a plain program's by a relative error of at most 0.0049.
Values may be sent and summed in bfloat16 or wider, within the bound.
A program may use at most 192 MiB of HBM per device.

v0:
```python
import jax
import jax.numpy as jnp
from jax import lax
from jax.sharding import PartitionSpec as P

BLOCK = 128


def body(hidden_rows, out_grad, expert_weights, need_lists, block_pick, owner_slot):
    groups = lax.axis_size("outer")
    members = lax.axis_size("dev")
    experts, row_count, col_count = expert_weights.shape
    need_count = need_lists.shape[1]
    token_count = hidden_rows.shape[0]
    feat_count = hidden_rows.shape[1]
    expert_ids = jnp.arange(experts, dtype=jnp.int32)
    matches = need_lists[:, :, None] == expert_ids[None, None, :]
    slot_table = jnp.sum(jnp.where(matches, owner_slot[None, None, :], 0), axis=2)
    slot_grid = slot_table.reshape(groups, members, need_count)
    pieces = expert_weights[slot_grid]
    moved = lax.all_to_all(
        lax.all_to_all(
            pieces.transpose(1, 0, 2, 3, 4), "dev", split_axis=0, concat_axis=0, tiled=True
        ),
        "outer",
        split_axis=1,
        concat_axis=1,
        tiled=True,
    )
    pulled = moved.transpose(2, 0, 3, 1, 4).reshape(
        need_count, members * row_count, groups * col_count
    )
    block_count = token_count // BLOCK
    forward_list = []
    backward_list = []
    for block in range(block_count):
        pick_now = block_pick[block]
        weight_now = lax.dynamic_index_in_dim(pulled, pick_now, 0, keepdims=False)
        block_hidden = hidden_rows[block * BLOCK : (block + 1) * BLOCK]
        block_grad = out_grad[block * BLOCK : (block + 1) * BLOCK]
        forward_list.append(
            jnp.dot(block_hidden, weight_now, preferred_element_type=jnp.float32).astype(
                jnp.bfloat16
            )
        )
        backward_list.append(
            lax.dot_general(
                block_grad, weight_now, (((1,), (1,)), ((), ())), preferred_element_type=jnp.float32
            ).astype(jnp.bfloat16)
        )
    layer_out = jnp.concatenate(forward_list, axis=0)
    hidden_grad = jnp.concatenate(backward_list, axis=0)
    hidden_blocks = hidden_rows.reshape(block_count, BLOCK, feat_count)
    partial_list = []
    for entry in range(need_count):
        keep = (block_pick == entry)[:, None, None]
        masked = jnp.where(keep, hidden_blocks, jnp.zeros((), jnp.bfloat16)).reshape(
            token_count, feat_count
        )
        product = lax.dot_general(
            masked, out_grad, (((0,), (0,)), ((), ())), preferred_element_type=jnp.float32
        )
        partial_list.append(product.astype(jnp.bfloat16))
    partial_value = jnp.stack(partial_list, axis=0)
    blocked = partial_value.reshape(need_count, members, row_count, groups, col_count)
    arrived = lax.all_to_all(
        lax.all_to_all(
            blocked.transpose(1, 3, 0, 2, 4), "outer", split_axis=1, concat_axis=1, tiled=True
        ),
        "dev",
        split_axis=0,
        concat_axis=0,
        tiled=True,
    )
    source_slots = slot_grid.transpose(1, 0, 2)
    selector = (source_slots.reshape(-1)[None, :] == expert_ids[:, None]).astype(jnp.bfloat16)
    summed = jnp.dot(
        selector, arrived.reshape(-1, row_count * col_count), preferred_element_type=jnp.float32
    )
    weight_grad = summed.astype(jnp.bfloat16).reshape(experts, row_count, col_count)
    return (layer_out, hidden_grad, weight_grad)


def solution(mesh):
    return jax.shard_map(
        body,
        mesh=mesh,
        in_specs=(
            P(("outer", "dev"), None),
            P(("outer", "dev"), None),
            P(None, "dev", "outer"),
            P(),
            P(("outer", "dev")),
            P(),
        ),
        out_specs=(P(("outer", "dev"), None), P(("outer", "dev"), None), P(None, "dev", "outer")),
        check_vma=False,
    )
```

profile of v0, /device:TPU:109, one launch (start us, length us, event | category | flops | bytes accessed | tf_op | source)
XLA Modules:
  0.0 1186.5 jit_solution(13948762707729146718)
XLA Ops:
  0.6 0.9 select_reduce_fusion
  2.1 51.2 %gather_fusion = bf16[512,12,1024]{2,0,1:T(8,128)(2,1)} fusion(bf16[64,12,1024]{2,0,1:T(8,128)(2,1)S(1)} %copy-done, s32[1024]{0:T(1024)S(1)} %pad_clamp_fusion), kind=kCustom, calls=%fused_computation | custom fusion | bytes 25167872 | tf_op jit(solution)/shard_map/gather | solution.py:20
  53.3 19.0 %reshape.69 = bf16[4,64,2,12,1024]{4,2,1,0,3:T(2,128)(2,1)} reshape(bf16[512,12,1024]{2,0,1:T(8,128)(2,1)} %gather_fusion) | data formatting | bytes 25165824 | tf_op jit(solution)/shard_map/gather | solution.py:20
  72.3 17.2 %copy.68 = bf16[4,64,2,12,1024]{4,0,3,2,1:T(4,128)(2,1)} copy(bf16[4,64,2,12,1024]{4,2,1,0,3:T(2,128)(2,1)} %reshape.69) | data formatting | bytes 25165824 | tf_op jit(solution)/shard_map/gather | solution.py:20
  89.5 9.9 all-to-all-start
  99.5 6.2 convolution_convert_fusion.1
  105.8 11.2 stack.10
  117.0 9.1 copy.59
  126.0 4.6 convolution_convert_fusion.2
  130.6 11.2 stack.9
  141.8 6.3 copy.58
  148.1 8.3 maximum_bitcast_fusion
  156.4 187.3 %all-to-all-done = bf16[64,4,2,12,1024]{4,1,3,2,0:T(4,128)(2,1)} async-done(((bf16[64,4,2,12,1024]{4,1,3,2,0:T(4,128)(2,1)}), bf16[64,4,2,12,1024]{4,1,3,2,0:T(4,128)(2,1)}, u32[]{:S(2)}, u32[]{:S(2)}) %all-to-all-start) | async-done | bytes 12582944 | tf_op jit(solution)/shard_map/all_to_all | solution.py:22
  343.7 6.7 all-to-all-start.2
  350.4 14.6 %copy.55 = bf16[64,4,2,12,1024]{4,0,3,2,1:T(8,128)(2,1)} copy(bf16[64,4,2,12,1024]{4,1,3,2,0:T(4,128)(2,1)} %all-to-all-done) | data formatting | bytes 25165824 | tf_op jit(solution)/shard_map/all_to_all | solution.py:22
  364.9 200.6 %all-to-all-done.2 = bf16[64,4,2,12,1024]{4,0,3,2,1:T(8,128)(2,1)} async-done(((bf16[64,4,2,12,1024]{4,0,3,2,1:T(8,128)(2,1)}), bf16[64,4,2,12,1024]{4,0,3,2,1:T(8,128)(2,1)}, u32[]{:S(2)}, u32[]{:S(2)}) %all-to-all-start.2) | async-done | bytes 12582944 | tf_op jit(solution)/shard_map/all_to_all | solution.py:67
  565.6 6.4 all-to-all-start.1
  572.0 17.3 %copy.60 = bf16[64,4,2,12,1024]{4,1,3,2,0:T(4,128)(2,1)} copy(bf16[64,4,2,12,1024]{4,0,3,2,1:T(8,128)(2,1)} %all-to-all-done.2) | data formatting | bytes 25165824 | tf_op jit(solution)/shard_map/all_to_all | solution.py:67
  589.2 165.7 %all-to-all-done.1 = bf16[64,4,2,12,1024]{4,0,3,2,1:T(8,128)(2,1)} async-done(((bf16[64,4,2,12,1024]{4,0,3,2,1:T(8,128)(2,1)}), bf16[64,4,2,12,1024]{4,0,3,2,1:T(8,128)(2,1)}, u32[]{:S(2)}, u32[]{:S(2)}) %all-to-all-start.1) | async-done | bytes 12582944 | tf_op jit(solution)/shard_map/all_to_all | solution.py:21
  754.9 219.6 %all-to-all-start.3 = ((bf16[64,4,2,12,1024]{4,1,3,2,0:T(4,128)(2,1)}), bf16[64,4,2,12,1024]{4,1,3,2,0:T(4,128)(2,1)}, u32[]{:S(2)}, u32[]{:S(2)}) async-start(bf16[64,4,2,12,1024]{4,1,3,2,0:T(4,128)(2,1)} %copy.60), calls=%async_computation.3 | async-start | bytes 25165824 | tf_op jit(solution)/shard_map/all_to_all | solution.py:66
  979.3 17.3 %copy.56 = bf16[2,64,12,4,1024]{4,3,2,1,0:T(4,128)(2,1)} copy(bf16[2,64,12,4,1024]{4,1,2,0,3:T(8,128)(2,1)} %bitcast.1) | data formatting | bytes 25165824 | tf_op jit(solution)/shard_map/transpose | solution.py:30
  996.6 21.0 %reshape.64 = bf16[2,768,4096]{2,1,0:T(8,128)(2,1)} reshape(bf16[2,64,12,4,1024]{4,3,2,1,0:T(4,128)(2,1)} %copy.56) | data formatting | bytes 25165824 | tf_op jit(solution)/shard_map/reshape | solution.py:30
  1017.7 3.9 fusion.18
  1021.6 5.5 fusion.21
  1027.2 2.2 fusion.33
  1029.4 2.2 fusion.30
  1031.6 118.8 %all-to-all-done.3 = bf16[64,4,2,12,1024]{4,1,3,2,0:T(4,128)(2,1)} async-done(((bf16[64,4,2,12,1024]{4,1,3,2,0:T(4,128)(2,1)}), bf16[64,4,2,12,1024]{4,1,3,2,0:T(4,128)(2,1)}, u32[]{:S(2)}, u32[]{:S(2)}) %all-to-all-start.3) | async-done | bytes 12582944 | tf_op jit(solution)/shard_map/all_to_all | solution.py:66
  1150.4 10.1 copy.61
  1160.5 19.7 %copy.65 = bf16[64,8,12,1024]{3,1,2,0:T(8,128)(2,1)S(1)} copy(bf16[64,8,12,1024]{3,2,1,0:T(8,128)(2,1)S(1)} %bitcast.66) | data formatting | bytes 25165824
  1180.2 2.3 convolution_convert_fusion
  1182.5 1.3 copy.69
  1184.6 1.5 pad_maximum_fusion
  (27 shorter events, 2.3 us)
Async XLA Ops:
  0.6 1.4 copy-start
  89.5 9.9 copy-start.7
  89.5 10.0 copy-start.6
  89.5 254.2 %all-to-all-start = ((bf16[64,4,2,12,1024]{4,1,3,2,0:T(4,128)(2,1)}), bf16[64,4,2,12,1024]{4,1,3,2,0:T(4,128)(2,1)}, u32[]{:S(2)}, u32[]{:S(2)}) async-start(bf16[64,4,2,12,1024]{4,1,3,2,0:T(4,128)(2,1)} %bitcast.68), calls=%async_computation | async-start | bytes 25165824 | tf_op jit(solution)/shard_map/all_to_all | solution.py:22
  117.0 9.1 copy-start.3
  343.7 221.9 %all-to-all-start.2 = ((bf16[64,4,2,12,1024]{4,0,3,2,1:T(8,128)(2,1)}), bf16[64,4,2,12,1024]{4,0,3,2,1:T(8,128)(2,1)}, u32[]{:S(2)}, u32[]{:S(2)}) async-start(bf16[64,4,2,12,1024]{4,0,3,2,1:T(8,128)(2,1)} %maximum_bitcast_fusion), calls=%async_computation.2 | async-start | bytes 25165824 | tf_op jit(solution)/shard_map/all_to_all | solution.py:67
  565.6 189.3 %all-to-all-start.1 = ((bf16[64,4,2,12,1024]{4,0,3,2,1:T(8,128)(2,1)}), bf16[64,4,2,12,1024]{4,0,3,2,1:T(8,128)(2,1)}, u32[]{:S(2)}, u32[]{:S(2)}) async-start(bf16[64,4,2,12,1024]{4,0,3,2,1:T(8,128)(2,1)} %copy.55), calls=%async_computation.1 | async-start | bytes 25165824 | tf_op jit(solution)/shard_map/all_to_all | solution.py:21
  754.9 395.6 %all-to-all-start.3 = ((bf16[64,4,2,12,1024]{4,1,3,2,0:T(4,128)(2,1)}), bf16[64,4,2,12,1024]{4,1,3,2,0:T(4,128)(2,1)}, u32[]{:S(2)}, u32[]{:S(2)}) async-start(bf16[64,4,2,12,1024]{4,1,3,2,0:T(4,128)(2,1)} %copy.60), calls=%async_computation.3 | async-start | bytes 25165824 | tf_op jit(solution)/shard_map/all_to_all | solution.py:66
  1017.7 9.5 copy-start.2
  1017.7 9.5 copy-start.4
  1180.2 4.4 copy-start.5
  1180.2 5.9 copy-start.1
where the time goes:
time: 1200 us; the launch traced here: 1190 us
  waiting for transfers between devices  672 us (56%)
  starting transfers between devices  243 us (20%)
  local copies, waits for them, and re-layouts  228 us (19%)
  matrix products  27 us (2%)
    all_to_all x1, starting transfers between devices, body(): lax.all_to_all(lax.all_to_all(blocked.transpose(1, 3, 0, 2, 4), 'outer',...  220 us
    all_to_all x1, waiting for transfers between devices, body(): lax.all_to_all(blocked.transpose(1, 3, 0, 2, 4), 'outer', split_axis=1, c...  201 us
    all_to_all x1, waiting for transfers between devices, body(): lax.all_to_all(pieces.transpose(1, 0, 2, 3, 4), 'dev', split_axis=0, conc...  187 us
    all_to_all x1, waiting for transfers between devices, body(): lax.all_to_all(lax.all_to_all(pieces.transpose(1, 0, 2, 3, 4), 'dev', spl...  166 us
    all_to_all x1, waiting for transfers between devices, body(): lax.all_to_all(lax.all_to_all(blocked.transpose(1, 3, 0, 2, 4), 'outer',...  119 us
    gather x3, local copies, waits for them, and re-layouts, body(): pieces = expert_weights[slot_grid]  87.4 us
    another operation x4, local copies, waits for them, and re-layouts, body(): partial_value = jnp.stack(partial_list, axis=0)  37.7 us
  transfers between devices with their start and end apart: 4, of which 4 were waited for; matrix products, arithmetic and copies ran while one was open for 12% of the time, Pallas kernels for 0%

commit v1 on v0

v1 whole, which is shorter than its diff:
```python
import functools

import jax
import jax.numpy as jnp
from jax import lax
from jax.experimental import pallas as pl
from jax.experimental.pallas import tpu as pltpu
from jax.sharding import PartitionSpec as P

MESH = pl.DeviceIdType.MESH
BLOCK = 128
NX, NY, NZ, NC = 4, 4, 8, 2
ROWS = 12
GROUP = 192
COLS = 256
TOK = 256
EXPERTS = 64
VMEM_LIMIT = 60 * 2**20
OFFSETS = [(dz, dc) for dz in (0, 1, -1, 2, -2, 3, -3, 4) for dc in (0, 1)]


def coords():
    o, d = lax.axis_index("outer"), lax.axis_index("dev")
    return d // 16, (d // 2) % 4, o * 2 + (d // 8) % 2, d % 2


def device(x, y, z, c):
    return (z // 2, x * 16 + (z % 2) * 8 + y * 2 + c)


class Copies:
    def __init__(self, send, recv):
        self.send, self.recv, self.used, self.pending = send, recv, 0, []

    def start(self, src, dst, target, land):
        n = self.used
        self.used += 1
        copy = pltpu.make_async_remote_copy(src, dst, self.send.at[n], self.recv.at[n], device_id=target, device_id_type=MESH)
        copy.start()
        self.pending.append(copy)
        back = pltpu.make_async_remote_copy(land, land, self.send.at[n], self.recv.at[n], device_id=target, device_id_type=MESH)
        return back

    def local(self, src, dst):
        n = self.used
        self.used += 1
        copy = pltpu.make_async_copy(src, dst, self.recv.at[n])
        copy.start()
        return copy

    def drain(self):
        for copy in self.pending:
            copy.wait_send()


def greet(x, y, z, c):
    barrier = pltpu.get_barrier_semaphore()
    others = [(x, y, (z + dz + NZ) % NZ, (c + dc) % 2) for dz, dc in OFFSETS[1:]]
    others += [(x, (y + dy) % NY, z, c) for dy in (1, 2, 3)]
    others += [((x + dx) % NX, y, z, c) for dx in (1, 3)]
    for other in others:
        pl.semaphore_signal(barrier, inc=1, device_id=device(*other), device_id_type=MESH)
    pl.semaphore_wait(barrier, len(others))


def quarter(q):
    return pl.ds(pl.multiple_of(q * COLS, COLS), COLS)


def gather_kernel(w, h, g, wg, hg, gg, send, recv):
    x, y, z, c = coords()
    greet(x, y, z, c)
    cp = Copies(send, recv)
    zof = lambda d: (z + d + NZ) % NZ
    yof = lambda d: (y + d + NY) % NY
    xof = lambda d: (x + d + NX) % NX
    zl = z % 2
    here = zl * 2 + c

    w1 = []
    for dl, dc in ((0, 1), (1, 0), (1, 1)):
        ol, oc = (zl + dl) % 2, (c + dc) % 2
        there = ol * 2 + oc
        w1.append(cp.start(w.at[:, :, quarter(there)], wg.at[x, here], device(x, y, (z // 2) * 2 + ol, oc), wg.at[x, there]))
    w1.append(cp.local(w.at[:, :, quarter(here)], wg.at[x, here]))
    h1 = []
    for dy in (1, 3, 2):
        oy = yof(dy)
        h1.append(cp.start(h.at[oy], hg.at[z, c, y], device(x, oy, z, c), hg.at[z, c, yof(-dy)]))
    h1.append(cp.local(h.at[y], hg.at[z, c, y]))
    g1 = []
    for dz, dc in OFFSETS:
        if (dz, dc) == (0, 0):
            g1.append(cp.local(g.at[:, quarter(z * 2 + c)], gg.at[z, c, y]))
            continue
        oz, oc = zof(dz), (c + dc) % 2
        g1.append(cp.start(g.at[:, quarter(oz * 2 + oc)], gg.at[z, c, y], device(x, y, oz, oc), gg.at[zof(-dz), oc, y]))

    def wait(copy):
        if hasattr(copy, "wait_recv") and copy.is_remote:
            copy.wait_recv()
        else:
            copy.wait()

    up_z, down_z = device(x, y, zof(1), c), device(x, y, zof(-1), c)
    up_y, down_y = device(x, yof(1), z, c), device(x, yof(-1), z, c)
    up_x, down_x = device(xof(1), y, z, c), device(xof(-1), y, z, c)
    sibling = device(x, y, z, (c + 1) % 2)

    h_state = {}
    h_sib = []

    def h_step(s):
        if s == 0:
            for copy in h1:
                wait(copy)
        else:
            wait(h_state["up"])
            wait(h_state["down"])
        behind, ahead = zof(-s), zof(s)
        if s < 3:
            h_state["up"] = cp.start(hg.at[behind, c], hg.at[behind, c], up_z, hg.at[zof(-s - 1), c])
            h_state["down"] = cp.start(hg.at[ahead, c], hg.at[ahead, c], down_z, hg.at[zof(s + 1), c])
        elif s == 3:
            h_state["up"] = cp.start(hg.at[behind, c, 0:2], hg.at[behind, c, 0:2], up_z, hg.at[zof(-4), c, 0:2])
            h_state["down"] = cp.start(hg.at[ahead, c, 2:4], hg.at[ahead, c, 2:4], down_z, hg.at[zof(4), c, 2:4])
        for zz in [behind] if s in (0, 4) else [behind, ahead]:
            h_sib.append(cp.start(hg.at[zz, c], hg.at[zz, c], sibling, hg.at[zz, (c + 1) % 2]))

    w_state = {}

    def w_step(s):
        if s == 0:
            for copy in w1:
                wait(copy)
            w_state["up"] = cp.start(wg.at[x], wg.at[x], up_x, wg.at[xof(-1)])
            w_state["down"] = cp.start(wg.at[x], wg.at[x], down_x, wg.at[xof(1)])
        else:
            wait(w_state["up"])
            wait(w_state["down"])
            if s == 1:
                w_state["up"] = cp.start(wg.at[xof(-1), 0:2], wg.at[xof(-1), 0:2], up_x, wg.at[xof(-2), 0:2])
                w_state["down"] = cp.start(wg.at[xof(1), 2:4], wg.at[xof(1), 2:4], down_x, wg.at[xof(2), 2:4])

    g2, g3 = [], []
    half = TOK // 2

    def g_first(k):
        wait(g1[k])
        dz, dc = OFFSETS[k]
        zs, cs = zof(-dz), (c + dc) % 2
        mine = gg.at[zs, cs, y]
        g2.append((cp.start(mine, mine, up_y, gg.at[zs, cs, yof(-1)]), cp.start(mine, mine, down_y, gg.at[zs, cs, yof(1)])))

    def g_second(k):
        dz, dc = OFFSETS[k]
        zs, cs = zof(-dz), (c + dc) % 2
        for copy in g2[k]:
            wait(copy)
        below = gg.at[zs, cs, yof(-1), 0:half]
        above = gg.at[zs, cs, yof(1), half:TOK]
        g3.append(cp.start(below, below, up_y, gg.at[zs, cs, yof(-2), 0:half]))
        g3.append(cp.start(above, above, down_y, gg.at[zs, cs, yof(2), half:TOK]))

    g_first(0)
    h_step(0)
    w_step(0)
    steps = len(OFFSETS)
    for k in range(1, steps):
        g_first(k)
        if k >= 2:
            g_second(k - 2)
        if k in (4, 7, 10, 13):
            h_step((k - 1) // 3)
        if k == 8:
            w_step(1)
    g_second(steps - 2)
    g_second(steps - 1)
    w_step(2)
    for copy in g3 + h_sib:
        wait(copy)
    cp.drain()


def compute_kernel(slots, w, h, g, lo, hgrad, dw, wf, acc):
    step = pl.program_id(0)
    lanes = [slice(j * 128, (j + 1) * 128) for j in range(COLS // 128)]

    @pl.when(step == 0)
    def _():
        def fill(i, carry):
            rows = pl.ds(pl.multiple_of(i * 256, 256), 256)
            for j, lane in enumerate(lanes):
                wf[j, rows, :] = w[rows, lane].astype(jnp.float32)
                acc[j, rows, :] = jnp.zeros((256, 128), jnp.float32)
            return carry

        lax.fori_loop(0, GROUP * EXPERTS // 256, fill, 0)

    for b in range(TOK // BLOCK):
        slot = slots[step * (TOK // BLOCK) + b]
        rows = pl.ds(slot, GROUP, stride=EXPERTS)
        weight = jnp.concatenate([wf[j, rows, :] for j in range(len(lanes))], axis=1).astype(jnp.bfloat16)
        tokens = slice(b * BLOCK, (b + 1) * BLOCK)
        hid = h[0, :, tokens]
        cot = g[0, tokens, :]
        lo[0, tokens, :] = lax.dot_general(
            hid, weight, (((0,), (0,)), ((), ())), preferred_element_type=jnp.float32
        ).astype(jnp.bfloat16)
        hgrad[0, :, tokens] = lax.dot_general(
            weight, cot, (((1,), (1,)), ((), ())), preferred_element_type=jnp.float32
        ).astype(jnp.bfloat16)
        outer = jnp.dot(hid, cot, preferred_element_type=jnp.float32)
        for j, lane in enumerate(lanes):
            acc[j, rows, :] += outer[:, lane]

    @pl.when(step == pl.num_programs(0) - 1)
    def _():
        def empty(i, carry):
            rows = pl.ds(pl.multiple_of(i * 256, 256), 256)
            for j, lane in enumerate(lanes):
                dw[rows, lane] = acc[j, rows, :].astype(jnp.bfloat16)
            return carry

        lax.fori_loop(0, GROUP * EXPERTS // 256, empty, 0)


def add_into(dst, *others):
    lead = dst.shape[:-2]
    rows = dst.shape[-2]
    cut = 64
    per = rows // cut
    total = per
    for n in lead:
        total *= n

    def one(i, carry):
        where, rest = [], i // per
        for n in reversed(lead):
            where.insert(0, rest % n)
            rest = rest // n
        at = tuple(where) + (pl.ds(pl.multiple_of((i % per) * cut, cut), cut), slice(None))
        value = dst[at].astype(jnp.float32)
        for other in others:
            value += other[at].astype(jnp.float32)
        dst[at] = value.astype(jnp.bfloat16)
        return carry

    lax.fori_loop(0, total, one, 0)


def scatter_kernel(lo, hp, dw, out, hout, wout, lo_half_up, lo_half_dn, lo_up, lo_dn, sib, hp_up, hp_dn, dw_half_up, dw_half_dn, dw_up, dw_dn, send, recv):
    x, y, z, c = coords()
    greet(x, y, z, c)
    cp = Copies(send, recv)
    zof = lambda d: (z + d + NZ) % NZ
    yof = lambda d: (y + d + NY) % NY
    xof = lambda d: (x + d + NX) % NX
    zl = z % 2
    here = zl * 2 + c
    up_z, down_z = device(x, y, zof(1), c), device(x, y, zof(-1), c)
    up_y, down_y = device(x, yof(1), z, c), device(x, yof(-1), z, c)
    up_x, down_x = device(xof(1), y, z, c), device(xof(-1), y, z, c)
    sibling = device(x, y, z, (c + 1) % 2)
    half = TOK // 2
    order = list(reversed(OFFSETS))

    sib_in = {}
    for d in (4, 3, -3, 2, -2, 1, -1, 0):
        zz = zof(d)
        sib_in[d] = cp.start(hp.at[zz, (c + 1) % 2], sib.at[zz], sibling, sib.at[zz])
    a_in = []
    for k, (dz, dc) in enumerate(order):
        zs, cs = zof(dz), (c + dc) % 2
        a_in.append((
            cp.start(lo.at[zs, cs, yof(2), 0:half], lo_half_up.at[k], up_y, lo_half_up.at[k]),
            cp.start(lo.at[zs, cs, yof(2), half:TOK], lo_half_dn.at[k], down_y, lo_half_dn.at[k]),
        ))
    d_in = (
        cp.start(dw.at[xof(2), 0:2], dw_half_up, up_x, dw_half_up),
        cp.start(dw.at[xof(2), 2:4], dw_half_dn, down_x, dw_half_dn),
    )

    h_state = {}

    def h_step(s):
        for d in (4,) if s == 4 else (s, -s) if s else (0,):
            sib_in[d].wait_recv()
        if s < 4:
            h_state["up"].wait_recv()
            h_state["down"].wait_recv()
        if s == 4:
            add_into(hp.at[zof(4), c], sib.at[zof(4)])
            h_state["up"] = cp.start(hp.at[zof(4), c, 0:2], hp_up.at[3, 0:2], up_z, hp_up.at[3, 0:2])
            h_state["down"] = cp.start(hp.at[zof(4), c, 2:4], hp_dn.at[3, 2:4], down_z, hp_dn.at[3, 2:4])
            return
        if s == 3:
            add_into(hp.at[zof(3), c, 0:2], sib.at[zof(3), 0:2], hp_up.at[3, 0:2])
            add_into(hp.at[zof(3), c, 2:4], sib.at[zof(3), 2:4])
            add_into(hp.at[zof(-3), c, 0:2], sib.at[zof(-3), 0:2])
            add_into(hp.at[zof(-3), c, 2:4], sib.at[zof(-3), 2:4], hp_dn.at[3, 2:4])
        elif s > 0:
            add_into(hp.at[zof(s), c], sib.at[zof(s)], hp_up.at[s])
            add_into(hp.at[zof(-s), c], sib.at[zof(-s)], hp_dn.at[s])
        else:
            add_into(hp.at[z, c], sib.at[z], hp_up.at[0], hp_dn.at[0])
        if s > 0:
            h_state["up"] = cp.start(hp.at[zof(s), c], hp_up.at[s - 1], up_z, hp_up.at[s - 1])
            h_state["down"] = cp.start(hp.at[zof(-s), c], hp_dn.at[s - 1], down_z, hp_dn.at[s - 1])

    b_in, o_in = [], []

    def lo_second(k):
        dz, dc = order[k]
        zs, cs = zof(dz), (c + dc) % 2
        a_in[k][0].wait_recv()
        add_into(lo.at[zs, cs, yof(1), 0:half], lo_half_up.at[k])
        first = cp.start(lo.at[zs, cs, yof(1)], lo_up.at[k], up_y, lo_up.at[k])
        a_in[k][1].wait_recv()
        add_into(lo.at[zs, cs, yof(-1), half:TOK], lo_half_dn.at[k])
        b_in.append((first, cp.start(lo.at[zs, cs, yof(-1)], lo_dn.at[k], down_y, lo_dn.at[k])))

    def lo_third(k):
        dz, dc = order[k]
        zs, cs = zof(dz), (c + dc) % 2
        for copy in b_in[k]:
            copy.wait_recv()
        add_into(lo.at[zs, cs, y], lo_up.at[k], lo_dn.at[k])
        mine = out.at[:, quarter(z * 2 + c)]
        if (dz, dc) == (0, 0):
            o_in.append(cp.local(lo.at[zs, cs, y], mine))
        else:
            o_in.append(cp.start(lo.at[zs, cs, y], mine, device(x, y, zs, cs), out.at[:, quarter(zof(-dz) * 2 + cs)]))

    d_state = {}

    def d_step(s):
        if s == 0:
            d_in[0].wait_recv()
            add_into(dw.at[xof(1), 0:2], dw_half_up)
            d_state["up"] = cp.start(dw.at[xof(1)], dw_up, up_x, dw_up)
            d_in[1].wait_recv()
            add_into(dw.at[xof(-1), 2:4], dw_half_dn)
            d_state["down"] = cp.start(dw.at[xof(-1)], dw_dn, down_x, dw_dn)
            return
        d_state["up"].wait_recv()
        d_state["down"].wait_recv()
        add_into(dw.at[x], dw_up, dw_dn)
        for dl, dc in ((1, 0), (1, 1), (0, 1)):
            ol, oc = (zl + dl) % 2, (c + dc) % 2
            there = ol * 2 + oc
            o_in.append(cp.start(dw.at[x, there], wout.at[:, :, quarter(here)], device(x, y, (z // 2) * 2 + ol, oc), wout.at[:, :, quarter(there)]))
        o_in.append(cp.local(dw.at[x, here], wout.at[:, :, quarter(here)]))

    h_step(4)
    steps = len(order)
    for k in range(steps):
        lo_second(k)
        if k >= 2:
            lo_third(k - 2)
        if k in (3, 6, 9, 12):
            h_step(4 - k // 3)
        if k == 4:
            d_step(0)
        if k == 10:
            d_step(1)
    for dy in (1, 3, 2):
        oy = yof(dy)
        o_in.append(cp.start(hp.at[z, c, oy], hout.at[y], device(x, oy, z, c), hout.at[yof(-dy)]))
    o_in.append(cp.local(hp.at[z, c, y], hout.at[y]))
    lo_third(steps - 2)
    lo_third(steps - 1)
    for copy in o_in:
        if copy.is_remote:
            copy.wait_recv()
        else:
            copy.wait()
    cp.drain()


def body(hidden_rows, out_grad, expert_weights, need_lists, block_pick, owner_slot):
    bf16 = jnp.bfloat16
    shape = jax.ShapeDtypeStruct
    anywhere = pl.BlockSpec(memory_space=pl.ANY)
    vmem = pl.BlockSpec(memory_space=pltpu.VMEM)
    x = lax.axis_index("dev") // 16

    picks = lax.all_gather(block_pick, ("outer", "dev"), axis=0, tiled=True).reshape(256, 2)
    experts = jnp.where(picks == 0, need_lists[:, 0:1], need_lists[:, 1:2])
    ids = jnp.arange(EXPERTS, dtype=jnp.int32)
    slots = jnp.sum(jnp.where(experts[:, :, None] == ids, owner_slot[None, None, :], 0), axis=2)
    slots = slots.reshape(4, NX, 2, NY, NC, 2)
    slots = lax.dynamic_index_in_dim(slots, x, 1, keepdims=False).transpose(0, 1, 3, 2, 4).reshape(-1)

    ht = hidden_rows.reshape(TOK, NX, 2, NY, NC, ROWS).transpose(3, 1, 2, 4, 5, 0).reshape(NY, GROUP, TOK)
    wt = expert_weights.transpose(1, 0, 2)

    wg, hg, gg = pl.pallas_call(
        gather_kernel,
        out_shape=(
            shape((NX, 4, ROWS, EXPERTS, COLS), bf16),
            shape((NZ, NC, NY, GROUP, TOK), bf16),
            shape((NZ, NC, NY, TOK, COLS), bf16),
        ),
        in_specs=[anywhere] * 3,
        out_specs=(anywhere,) * 3,
        scratch_shapes=[pltpu.SemaphoreType.DMA((128,)), pltpu.SemaphoreType.DMA((128,))],
        compiler_params=pltpu.CompilerParams(collective_id=0, has_side_effects=True, vmem_limit_bytes=VMEM_LIMIT),
        name="gather",
    )(wt, ht, out_grad)

    sources = NZ * NC * NY
    one = lambda rows: pl.BlockSpec((1, rows, 256), lambda i, s: (i, 0, 0))
    whole = lambda: pl.BlockSpec((GROUP * EXPERTS, COLS), lambda i, s: (0, 0), pipeline_mode=pl.Buffered(1))
    lo, hp, dw = pl.pallas_call(
        compute_kernel,
        grid_spec=pltpu.PrefetchScalarGridSpec(
            num_scalar_prefetch=1,
            grid=(sources,),
            in_specs=[whole(), one(GROUP), one(TOK)],
            out_specs=(one(TOK), one(GROUP), whole()),
            scratch_shapes=[
                pltpu.VMEM((COLS // 128, GROUP * EXPERTS, 128), jnp.float32),
                pltpu.VMEM((COLS // 128, GROUP * EXPERTS, 128), jnp.float32),
            ],
        ),
        out_shape=(
            shape((sources, TOK, COLS), bf16),
            shape((sources, GROUP, TOK), bf16),
            shape((GROUP * EXPERTS, COLS), bf16),
        ),
        compiler_params=pltpu.CompilerParams(vmem_limit_bytes=VMEM_LIMIT),
        name="compute",
    )(slots, wg.reshape(GROUP * EXPERTS, COLS), hg.reshape(sources, GROUP, TOK), gg.reshape(sources, TOK, COLS))

    half = TOK // 2
    pieces = len(OFFSETS)
    layer_out, hidden, weight_grad = pl.pallas_call(
        scatter_kernel,
        out_shape=(
            shape((TOK, 4096), bf16),
            shape((NY, GROUP, TOK), bf16),
            shape((ROWS, EXPERTS, 1024), bf16),
        ),
        in_specs=[vmem] * 3,
        out_specs=(anywhere,) * 3,
        scratch_shapes=[
            pltpu.VMEM((pieces, half, COLS), bf16),
            pltpu.VMEM((pieces, half, COLS), bf16),
            pltpu.VMEM((pieces, TOK, COLS), bf16),
            pltpu.VMEM((pieces, TOK, COLS), bf16),
            pltpu.VMEM((NZ, NY, GROUP, TOK), bf16),
            pltpu.VMEM((4, NY, GROUP, TOK), bf16),
            pltpu.VMEM((4, NY, GROUP, TOK), bf16),
            pltpu.VMEM((2, ROWS, EXPERTS, COLS), bf16),
            pltpu.VMEM((2, ROWS, EXPERTS, COLS), bf16),
            pltpu.VMEM((4, ROWS, EXPERTS, COLS), bf16),
            pltpu.VMEM((4, ROWS, EXPERTS, COLS), bf16),
            pltpu.SemaphoreType.DMA((128,)),
            pltpu.SemaphoreType.DMA((128,)),
        ],
        compiler_params=pltpu.CompilerParams(collective_id=1, has_side_effects=True, vmem_limit_bytes=VMEM_LIMIT),
        name="scatter",
    )(
        lo.reshape(NZ, NC, NY, TOK, COLS),
        hp.reshape(NZ, NC, NY, GROUP, TOK),
        dw.reshape(NX, 4, ROWS, EXPERTS, COLS),
    )
    hidden_grad = hidden.reshape(NY, NX, 2, NC, ROWS, TOK).transpose(5, 1, 2, 0, 3, 4).reshape(TOK, -1)
    return layer_out, hidden_grad, weight_grad.transpose(1, 0, 2)


def solution(mesh):
    return jax.shard_map(
        body,
        mesh=mesh,
        in_specs=(
            P(("outer", "dev"), None),
            P(("outer", "dev"), None),
            P(None, "dev", "outer"),
            P(),
            P(("outer", "dev")),
            P(),
        ),
        out_specs=(P(("outer", "dev"), None), P(("outer", "dev"), None), P(None, "dev", "outer")),
        check_vma=False,
    )
```

time: 1200 us -> 451 us (0.38)
  the two profiles are of different devices: /device:TPU:109 before, /device:TPU:32 now
where the time goes in v1:
time: 451 us
  Pallas kernels  357 us (79%)
  blocking collectives  79.8 us (18%)
  local copies, waits for them, and re-layouts  12.2 us (3%)
    pallas_call x1, Pallas kernels, body(): pl.pallas_call(scatter_kernel, out_shape=(shape((TOK, 4096), bf16), shape...  131 us
    pallas_call x1, Pallas kernels, body(): pl.pallas_call(gather_kernel, out_shape=(shape((NX, 4, ROWS, EXPERTS, COL...  131 us
    pallas_call x1, Pallas kernels, body(): pl.pallas_call(compute_kernel, grid_spec=pltpu.PrefetchScalarGridSpec(num...  95.6 us
    unnamed x1, blocking collectives  79.8 us

profile of v1, /device:TPU:32, one launch (start us, length us, event | category | flops | bytes accessed | tf_op | source)
XLA Modules:
  0.0 450.9 jit_solution(17843710084583487538)
XLA Ops:
  0.7 0.9 dynamic-update-slice
  1.5 79.8 %all-reduce = s32[512]{0:T(512)S(1)} all-reduce(s32[512]{0:T(512)S(1)} %dynamic-update-slice), channel_id=1, replica_groups=mesh['outer'=4,'dev'=64] {'outer','dev'}, use_global_device_ids=true, to_apply=%add | all-reduce | flops 512 | bytes 4096
  81.3 0.8 fusion
  82.1 0.2 eq.28
  82.2 0.1 broadcast_select_fusion
  82.4 0.1 copy.20
  82.4 0.8 select_reduce_fusion
  83.2 0.2 reshape.84
  83.4 0.3 copy.22
  83.7 0.7 reshape.85.slots
  84.4 1.2 copy.23
  85.6 0.1 reshape.86
  85.7 0.3 copy.24
  86.0 0.8 copy.25.h
  86.8 130.8 %gather.1 = (bf16[4,4,12,64,256]{4,3,2,1,0:T(8,128)(2,1)}, bf16[8,2,4,192,256]{4,3,2,1,0:T(8,128)(2,1)}, bf16[8,2,4,256,256]{4,3,2,1,0:T(8,128)(2,1)}) custom-call(bf16[12,64,1024]{2,1,0:T(8,128)(2,1)} %bitcast.35, bf16[4,192,256]{2,1,0:T(8,128)(2,1)} %copy.25.h, bf16[256,4096]{1,0:T(8,128)(2,1)} %g.1), custom_call_target="tpu_custom_call" | custom-call | tf_op jit(solution)/shard_map/gather/pallas_call | solution.py:398
  217.5 95.6 %compute.1 = (bf16[64,256,256]{2,1,0:T(8,128)(2,1)}, bf16[64,192,256]{2,1,0:T(8,128)(2,1)}, bf16[12288,256]{1,0:T(8,128)(2,1)}) custom-call(s32[128]{0:T(128)} %reshape.85.slots, bf16[12288,256]{1,0:T(8,128)(2,1)} %bitcast.29, bf16[64,192,256]{2,1,0:T(8,128)(2,1)} %bitcast.30, bf16[64,256,256]{2,1,0:T(8,128)(2,1)} %bitcast.26), custom_call_target="tpu_custom_call" | custom-call | tf_op jit(solution)/shard_map/compute/pallas_call | solution.py:415
  313.2 130.9 %scatter.1 = (bf16[256,4096]{1,0:T(8,128)(2,1)}, bf16[4,192,256]{2,1,0:T(8,128)(2,1)}, bf16[12,64,1024]{2,1,0:T(8,128)(2,1)}) custom-call(bf16[8,2,4,256,256]{4,3,2,1,0:T(8,128)(2,1)} %bitcast.25, bf16[8,2,4,192,256]{4,3,2,1,0:T(8,128)(2,1)} %bitcast.27, bf16[4,4,12,64,256]{4,3,2,1,0:T(8,128)(2,1)} %bitcast.28), custom_call_target="tpu_custom_call" | custom-call | tf_op jit(solution)/shard_map/scatter/pallas_call | solution.py:438
  444.1 0.0 copy-start
  444.1 1.4 copy.26
  445.5 0.1 copy.27
  445.6 0.1 reshape.95
  445.7 0.9 copy.28
  446.6 3.1 copy.33
  449.7 0.0 copy-done
  449.7 1.1 copy.34
  (3 shorter events, 0.0 us)
Async XLA Ops:
  444.1 5.7 %copy-start = (bf16[12,64,1024]{2,1,0:T(8,128)(2,1)S(1)}, bf16[12,64,1024]{2,1,0:T(8,128)(2,1)}, u32[]{:S(2)}) copy-start(bf16[12,64,1024]{2,1,0:T(8,128)(2,1)} %get-tuple-element.20) | copy-start | bytes 4718596

commit v2 on v1

--- a/solution.py
+++ b/solution.py
@@ -67,7 +67,7 @@
     return pl.ds(pl.multiple_of(q * COLS, COLS), COLS)
 
 
-def gather_kernel(w, h, g, wg, hg, gg, send, recv):
+def gather_kernel(w, h, g, pick, wg, hg, gg, picks, landed, wide, turned, send, recv):
     x, y, z, c = coords()
     greet(x, y, z, c)
     cp = Copies(send, recv)
@@ -77,27 +77,32 @@
     zl = z % 2
     here = zl * 2 + c
 
-    w1 = []
-    for dl, dc in ((0, 1), (1, 0), (1, 1)):
-        ol, oc = (zl + dl) % 2, (c + dc) % 2
-        there = ol * 2 + oc
-        w1.append(cp.start(w.at[:, :, quarter(there)], wg.at[x, here], device(x, y, (z // 2) * 2 + ol, oc), wg.at[x, there]))
-    w1.append(cp.local(w.at[:, :, quarter(here)], wg.at[x, here]))
     h1 = []
     for dy in (1, 3, 2):
         oy = yof(dy)
         h1.append(cp.start(h.at[oy], hg.at[z, c, y], device(x, oy, z, c), hg.at[z, c, yof(-dy)]))
+        h1.append(cp.start(pick, picks.at[z, c, y], device(x, oy, z, c), picks.at[z, c, yof(-dy)]))
     h1.append(cp.local(h.at[y], hg.at[z, c, y]))
+    h1.append(cp.local(pick, picks.at[z, c, y]))
+    w1 = []
+    for dl, dc in ((1, 0), (1, 1), (0, 1)):
+        ol, oc = (zl + dl) % 2, (c + dc) % 2
+        there = ol * 2 + oc
+        w1.append(cp.start(w.at[:, :, quarter(there)], landed.at[here], device(x, y, (z // 2) * 2 + ol, oc), landed.at[there]))
+    w1.append(cp.local(w.at[:, :, quarter(here)], landed.at[here]))
+
     g1 = []
-    for dz, dc in OFFSETS:
+
+    def g_start(k):
+        dz, dc = OFFSETS[k]
         if (dz, dc) == (0, 0):
             g1.append(cp.local(g.at[:, quarter(z * 2 + c)], gg.at[z, c, y]))
-            continue
+            return
         oz, oc = zof(dz), (c + dc) % 2
         g1.append(cp.start(g.at[:, quarter(oz * 2 + oc)], gg.at[z, c, y], device(x, y, oz, oc), gg.at[zof(-dz), oc, y]))
 
     def wait(copy):
-        if hasattr(copy, "wait_recv") and copy.is_remote:
+        if copy.is_remote:
             copy.wait_recv()
         else:
             copy.wait()
@@ -107,40 +112,64 @@
     up_x, down_x = device(xof(1), y, z, c), device(xof(-1), y, z, c)
     sibling = device(x, y, z, (c + 1) % 2)
 
-    h_state = {}
+    h_state = []
     h_sib = []
 
+    def h_send(pairs, target, back):
+        for ref, at, land in pairs:
+            back.append(cp.start(ref.at[at], ref.at[at], target, ref.at[land]))
+
     def h_step(s):
-        if s == 0:
-            for copy in h1:
-                wait(copy)
-        else:
-            wait(h_state["up"])
-            wait(h_state["down"])
+        for copy in h1 if s == 0 else list(h_state):
+            wait(copy)
+        h_state.clear()
         behind, ahead = zof(-s), zof(s)
         if s < 3:
-            h_state["up"] = cp.start(hg.at[behind, c], hg.at[behind, c], up_z, hg.at[zof(-s - 1), c])
-            h_state["down"] = cp.start(hg.at[ahead, c], hg.at[ahead, c], down_z, hg.at[zof(s + 1), c])
+            h_send([(hg, (behind, c), (zof(-s - 1), c)), (picks, (behind, c), (zof(-s - 1), c))], up_z, h_state)
+            h_send([(hg, (ahead, c), (zof(s + 1), c)), (picks, (ahead, c), (zof(s + 1), c))], down_z, h_state)
         elif s == 3:
-            h_state["up"] = cp.start(hg.at[behind, c, 0:2], hg.at[behind, c, 0:2], up_z, hg.at[zof(-4), c, 0:2])
-            h_state["down"] = cp.start(hg.at[ahead, c, 2:4], hg.at[ahead, c, 2:4], down_z, hg.at[zof(4), c, 2:4])
+            low, high = slice(0, 2), slice(2, 4)
+            h_send([(hg, (behind, c, low), (zof(-4), c, low)), (picks, (behind, c, low), (zof(-4), c, low))], up_z, h_state)
+            h_send([(hg, (ahead, c, high), (zof(4), c, high)), (picks, (ahead, c, high), (zof(4), c, high))], down_z, h_state)
         for zz in [behind] if s in (0, 4) else [behind, ahead]:
-            h_sib.append(cp.start(hg.at[zz, c], hg.at[zz, c], sibling, hg.at[zz, (c + 1) % 2]))
+            h_send([(r, (zz, c), (zz, (c + 1) % 2)) for r in (hg, picks)], sibling, h_sib)
 
     w_state = {}
+    bf16 = jnp.bfloat16
+    span = ROWS * 4
 
     def w_step(s):
         if s == 0:
             for copy in w1:
                 wait(copy)
-            w_state["up"] = cp.start(wg.at[x], wg.at[x], up_x, wg.at[xof(-1)])
-            w_state["down"] = cp.start(wg.at[x], wg.at[x], down_x, wg.at[xof(1)])
+
+            def widen(i, carry):
+                q, r = i // ROWS, i % ROWS
+                rows = pl.ds(pl.multiple_of(i * EXPERTS, EXPERTS), EXPERTS)
+                for j in range(COLS // 128):
+                    wide[j, rows, :] = landed[q, r, :, j * 128 : (j + 1) * 128].astype(jnp.float32)
+                return carry
+
+            lax.fori_loop(0, span, widen, 0)
+
+            def turn(e, carry):
+                for j in range(COLS // 128):
+                    turned[e, :, j * 128 : (j + 1) * 128] = wide[j, pl.ds(e, span, stride=EXPERTS), :].astype(bf16)
+                return carry
+
+            lax.fori_loop(0, EXPERTS, turn, 0)
+            w_state["up"] = cp.start(turned, wg.at[x], up_x, wg.at[xof(-1)])
+            w_state["down"] = cp.start(turned, wg.at[x], down_x, wg.at[xof(1)])
+            w_state["own"] = cp.local(turned, wg.at[x])
         else:
             wait(w_state["up"])
             wait(w_state["down"])
             if s == 1:
-                w_state["up"] = cp.start(wg.at[xof(-1), 0:2], wg.at[xof(-1), 0:2], up_x, wg.at[xof(-2), 0:2])
-                w_state["down"] = cp.start(wg.at[xof(1), 2:4], wg.at[xof(1), 2:4], down_x, wg.at[xof(2), 2:4])
+                low, high = slice(0, EXPERTS // 2), slice(EXPERTS // 2, EXPERTS)
+                w_state["up"] = cp.start(wg.at[xof(-1), low], wg.at[xof(-1), low], up_x, wg.at[xof(-2), low])
+                w_state["down"] = cp.start(wg.at[xof(1), high], wg.at[xof(1), high], down_x, wg.at[xof(2), high])
+            else:
+                wait(w_state["own"])
 
     g2, g3 = [], []
     half = TOK // 2
@@ -162,14 +191,16 @@
         g3.append(cp.start(below, below, up_y, gg.at[zs, cs, yof(-2), 0:half]))
         g3.append(cp.start(above, above, down_y, gg.at[zs, cs, yof(2), half:TOK]))
 
+    steps = len(OFFSETS)
+    for k in range(steps):
+        g_start(k)
     g_first(0)
     h_step(0)
+    g_first(1)
     w_step(0)
-    steps = len(OFFSETS)
-    for k in range(1, steps):
+    for k in range(2, steps):
         g_first(k)
-        if k >= 2:
-            g_second(k - 2)
+        g_second(k - 2)
         if k in (4, 7, 10, 13):
             h_step((k - 1) // 3)
         if k == 8:
@@ -182,53 +213,50 @@
     cp.drain()
 
 
-def compute_kernel(slots, w, h, g, lo, hgrad, dw, wf, acc):
+def compute_kernel(slots, w, h, g, lo, hgrad, dw, acc):
     step = pl.program_id(0)
-    lanes = [slice(j * 128, (j + 1) * 128) for j in range(COLS // 128)]
+    span = ROWS * 4
 
     @pl.when(step == 0)
     def _():
-        def fill(i, carry):
-            rows = pl.ds(pl.multiple_of(i * 256, 256), 256)
-            for j, lane in enumerate(lanes):
-                wf[j, rows, :] = w[rows, lane].astype(jnp.float32)
-                acc[j, rows, :] = jnp.zeros((256, 128), jnp.float32)
+        def clear(e, carry):
+            for j in range(NX):
+                acc[j, e] = jnp.zeros((span, COLS), jnp.float32)
             return carry
 
-        lax.fori_loop(0, GROUP * EXPERTS // 256, fill, 0)
-
-    for b in range(TOK // BLOCK):
-        slot = slots[step * (TOK // BLOCK) + b]
-        rows = pl.ds(slot, GROUP, stride=EXPERTS)
-        weight = jnp.concatenate([wf[j, rows, :] for j in range(len(lanes))], axis=1).astype(jnp.bfloat16)
-        tokens = slice(b * BLOCK, (b + 1) * BLOCK)
-        hid = h[0, :, tokens]
-        cot = g[0, tokens, :]
-        lo[0, tokens, :] = lax.dot_general(
-            hid, weight, (((0,), (0,)), ((), ())), preferred_element_type=jnp.float32
-        ).astype(jnp.bfloat16)
-        hgrad[0, :, tokens] = lax.dot_general(
-            weight, cot, (((1,), (1,)), ((), ())), preferred_element_type=jnp.float32
-        ).astype(jnp.bfloat16)
-        outer = jnp.dot(hid, cot, preferred_element_type=jnp.float32)
-        for j, lane in enumerate(lanes):
-            acc[j, rows, :] += outer[:, lane]
+        lax.fori_loop(0, EXPERTS, clear, 0)
+
+    for n in range(h.shape[0]):
+        for b in range(TOK // BLOCK):
+            slot = slots[(step * h.shape[0] + n) * (TOK // BLOCK) + b]
+            weight = jnp.concatenate([w[j, slot] for j in range(NX)], axis=0)
+            tokens = slice(b * BLOCK, (b + 1) * BLOCK)
+            hid = h[n, :, tokens]
+            cot = g[n, tokens, :]
+            lo[n, tokens, :] = lax.dot_general(
+                hid, weight, (((0,), (0,)), ((), ())), preferred_element_type=jnp.float32
+            ).astype(jnp.bfloat16)
+            hgrad[n, :, tokens] = lax.dot_general(
+                weight, cot, (((1,), (1,)), ((), ())), preferred_element_type=jnp.float32
+            ).astype(jnp.bfloat16)
+            outer = jnp.dot(hid, cot, preferred_element_type=jnp.float32)
+            for j in range(NX):
+                acc[j, slot] += outer[j * span : (j + 1) * span]
 
     @pl.when(step == pl.num_programs(0) - 1)
     def _():
-        def empty(i, carry):
-            rows = pl.ds(pl.multiple_of(i * 256, 256), 256)
-            for j, lane in enumerate(lanes):
-                dw[rows, lane] = acc[j, rows, :].astype(jnp.bfloat16)
+        def empty(e, carry):
+            for j in range(NX):
+                dw[j, e] = acc[j, e].astype(jnp.bfloat16)
             return carry
 
-        lax.fori_loop(0, GROUP * EXPERTS // 256, empty, 0)
+        lax.fori_loop(0, EXPERTS, empty, 0)
 
 
 def add_into(dst, *others):
     lead = dst.shape[:-2]
     rows = dst.shape[-2]
-    cut = 64
+    cut = min(rows, 64)
     per = rows // cut
     total = per
     for n in lead:
@@ -249,7 +277,7 @@
     lax.fori_loop(0, total, one, 0)
 
 
-def scatter_kernel(lo, hp, dw, out, hout, wout, lo_half_up, lo_half_dn, lo_up, lo_dn, sib, hp_up, hp_dn, dw_half_up, dw_half_dn, dw_up, dw_dn, send, recv):
+def scatter_kernel(lo, hp, dw, out, hout, wout, lo_half_up, lo_half_dn, lo_up, lo_dn, sib, hp_up, hp_dn, dw_half_up, dw_half_dn, dw_up, dw_dn, wide, turned, send, recv):
     x, y, z, c = coords()
     greet(x, y, z, c)
     cp = Copies(send, recv)
@@ -277,8 +305,8 @@
             cp.start(lo.at[zs, cs, yof(2), half:TOK], lo_half_dn.at[k], down_y, lo_half_dn.at[k]),
         ))
     d_in = (
-        cp.start(dw.at[xof(2), 0:2], dw_half_up, up_x, dw_half_up),
-        cp.start(dw.at[xof(2), 2:4], dw_half_dn, down_x, dw_half_dn),
+        cp.start(dw.at[xof(2), 0 : EXPERTS // 2], dw_half_up, up_x, dw_half_up),
+        cp.start(dw.at[xof(2), EXPERTS // 2 : EXPERTS], dw_half_dn, down_x, dw_half_dn),
     )
 
     h_state = {}
@@ -337,20 +365,36 @@
     def d_step(s):
         if s == 0:
             d_in[0].wait_recv()
-            add_into(dw.at[xof(1), 0:2], dw_half_up)
+            add_into(dw.at[xof(1), 0 : EXPERTS // 2], dw_half_up)
             d_state["up"] = cp.start(dw.at[xof(1)], dw_up, up_x, dw_up)
             d_in[1].wait_recv()
-            add_into(dw.at[xof(-1), 2:4], dw_half_dn)
+            add_into(dw.at[xof(-1), EXPERTS // 2 : EXPERTS], dw_half_dn)
             d_state["down"] = cp.start(dw.at[xof(-1)], dw_dn, down_x, dw_dn)
             return
         d_state["up"].wait_recv()
         d_state["down"].wait_recv()
-        add_into(dw.at[x], dw_up, dw_dn)
+        span = ROWS * 4
+
+        def turn(e, carry):
+            value = dw[x, e].astype(jnp.float32) + dw_up[e].astype(jnp.float32) + dw_dn[e].astype(jnp.float32)
+            for j in range(COLS // 128):
+                wide[j, pl.ds(e, span, stride=EXPERTS), :] = value[:, j * 128 : (j + 1) * 128]
+            return carry
+
+        lax.fori_loop(0, EXPERTS, turn, 0)
+
+        def narrow(i, carry):
+            rows = pl.ds(pl.multiple_of(i * EXPERTS, EXPERTS), EXPERTS)
+            for j in range(COLS // 128):
+                turned[i // ROWS, i % ROWS, :, j * 128 : (j + 1) * 128] = wide[j, rows, :].astype(jnp.bfloat16)
+            return carry
+
+        lax.fori_loop(0, span, narrow, 0)
         for dl, dc in ((1, 0), (1, 1), (0, 1)):
             ol, oc = (zl + dl) % 2, (c + dc) % 2
             there = ol * 2 + oc
-            o_in.append(cp.start(dw.at[x, there], wout.at[:, :, quarter(here)], device(x, y, (z // 2) * 2 + ol, oc), wout.at[:, :, quarter(there)]))
-        o_in.append(cp.local(dw.at[x, here], wout.at[:, :, quarter(here)]))
+            o_in.append(cp.start(turned.at[there], wout.at[:, :, quarter(here)], device(x, y, (z // 2) * 2 + ol, oc), wout.at[:, :, quarter(there)]))
+        o_in.append(cp.local(turned.at[here], wout.at[:, :, quarter(here)]))
 
     h_step(4)
     steps = len(order)
@@ -385,53 +429,60 @@
     vmem = pl.BlockSpec(memory_space=pltpu.VMEM)
     x = lax.axis_index("dev") // 16
 
-    picks = lax.all_gather(block_pick, ("outer", "dev"), axis=0, tiled=True).reshape(256, 2)
-    experts = jnp.where(picks == 0, need_lists[:, 0:1], need_lists[:, 1:2])
-    ids = jnp.arange(EXPERTS, dtype=jnp.int32)
-    slots = jnp.sum(jnp.where(experts[:, :, None] == ids, owner_slot[None, None, :], 0), axis=2)
-    slots = slots.reshape(4, NX, 2, NY, NC, 2)
-    slots = lax.dynamic_index_in_dim(slots, x, 1, keepdims=False).transpose(0, 1, 3, 2, 4).reshape(-1)
-
+    span = ROWS * 4
     ht = hidden_rows.reshape(TOK, NX, 2, NY, NC, ROWS).transpose(3, 1, 2, 4, 5, 0).reshape(NY, GROUP, TOK)
     wt = expert_weights.transpose(1, 0, 2)
-
-    wg, hg, gg = pl.pallas_call(
+    pick = jnp.broadcast_to(jnp.pad(block_pick, (0, 126))[None, :], (8, 128))
+
+    wg, hg, gg, picks = pl.pallas_call(
         gather_kernel,
         out_shape=(
-            shape((NX, 4, ROWS, EXPERTS, COLS), bf16),
+            shape((NX, EXPERTS, span, COLS), bf16),
             shape((NZ, NC, NY, GROUP, TOK), bf16),
             shape((NZ, NC, NY, TOK, COLS), bf16),
+            shape((NZ, NC, NY, 8, 128), jnp.int32),
         ),
-        in_specs=[anywhere] * 3,
-        out_specs=(anywhere,) * 3,
-        scratch_shapes=[pltpu.SemaphoreType.DMA((128,)), pltpu.SemaphoreType.DMA((128,))],
+        in_specs=[anywhere] * 4,
+        out_specs=(anywhere,) * 4,
+        scratch_shapes=[
+            pltpu.VMEM((4, ROWS, EXPERTS, COLS), bf16),
+            pltpu.VMEM((COLS // 128, span * EXPERTS, 128), jnp.float32),
+            pltpu.VMEM((EXPERTS, span, COLS), bf16),
+            pltpu.SemaphoreType.DMA((160,)),
+            pltpu.SemaphoreType.DMA((160,)),
+        ],
         compiler_params=pltpu.CompilerParams(collective_id=0, has_side_effects=True, vmem_limit_bytes=VMEM_LIMIT),
         name="gather",
-    )(wt, ht, out_grad)
+    )(wt, ht, out_grad, pick)
+
+    needs = need_lists.reshape(4, NX, 2, NY, NC, 2)
+    needs = lax.dynamic_index_in_dim(needs, x, 1, keepdims=False).transpose(0, 1, 3, 2, 4).reshape(-1, 2)
+    ids = jnp.arange(EXPERTS, dtype=jnp.int32)
+    known = jnp.sum(jnp.where(needs[:, :, None] == ids, owner_slot[None, None, :], 0), axis=2)
+    chosen = picks.reshape(-1, 8, 128)[:, 0, 0:2]
+    slots = jnp.where(chosen == 0, known[:, 0:1], known[:, 1:2]).reshape(-1)
 
     sources = NZ * NC * NY
-    one = lambda rows: pl.BlockSpec((1, rows, 256), lambda i, s: (i, 0, 0))
-    whole = lambda: pl.BlockSpec((GROUP * EXPERTS, COLS), lambda i, s: (0, 0), pipeline_mode=pl.Buffered(1))
+    each = 1
+    one = lambda rows: pl.BlockSpec((each, rows, 256), lambda i, s: (i, 0, 0))
+    whole = lambda: pl.BlockSpec((NX, EXPERTS, span, COLS), lambda i, s: (0, 0, 0, 0), pipeline_mode=pl.Buffered(1))
     lo, hp, dw = pl.pallas_call(
         compute_kernel,
         grid_spec=pltpu.PrefetchScalarGridSpec(
             num_scalar_prefetch=1,
-            grid=(sources,),
+            grid=(sources // each,),
             in_specs=[whole(), one(GROUP), one(TOK)],
             out_specs=(one(TOK), one(GROUP), whole()),
-            scratch_shapes=[
-                pltpu.VMEM((COLS // 128, GROUP * EXPERTS, 128), jnp.float32),
-                pltpu.VMEM((COLS // 128, GROUP * EXPERTS, 128), jnp.float32),
-            ],
+            scratch_shapes=[pltpu.VMEM((NX, EXPERTS, span, COLS), jnp.float32)],
         ),
         out_shape=(
             shape((sources, TOK, COLS), bf16),
             shape((sources, GROUP, TOK), bf16),
-            shape((GROUP * EXPERTS, COLS), bf16),
+            shape((NX, EXPERTS, span, COLS), bf16),
         ),
         compiler_params=pltpu.CompilerParams(vmem_limit_bytes=VMEM_LIMIT),
         name="compute",
-    )(slots, wg.reshape(GROUP * EXPERTS, COLS), hg.reshape(sources, GROUP, TOK), gg.reshape(sources, TOK, COLS))
+    )(slots, wg, hg.reshape(sources, GROUP, TOK), gg.reshape(sources, TOK, COLS))
 
     half = TOK // 2
     pieces = len(OFFSETS)
@@ -452,9 +503,11 @@
             pltpu.VMEM((NZ, NY, GROUP, TOK), bf16),
             pltpu.VMEM((4, NY, GROUP, TOK), bf16),
             pltpu.VMEM((4, NY, GROUP, TOK), bf16),
-            pltpu.VMEM((2, ROWS, EXPERTS, COLS), bf16),
-            pltpu.VMEM((2, ROWS, EXPERTS, COLS), bf16),
-            pltpu.VMEM((4, ROWS, EXPERTS, COLS), bf16),
+            pltpu.VMEM((EXPERTS // 2, span, COLS), bf16),
+            pltpu.VMEM((EXPERTS // 2, span, COLS), bf16),
+            pltpu.VMEM((EXPERTS, span, COLS), bf16),
+            pltpu.VMEM((EXPERTS, span, COLS), bf16),
+            pltpu.VMEM((COLS // 128, span * EXPERTS, 128), jnp.float32),
             pltpu.VMEM((4, ROWS, EXPERTS, COLS), bf16),
             pltpu.SemaphoreType.DMA((128,)),
             pltpu.SemaphoreType.DMA((128,)),
@@ -464,7 +517,7 @@
     )(
         lo.reshape(NZ, NC, NY, TOK, COLS),
         hp.reshape(NZ, NC, NY, GROUP, TOK),
-        dw.reshape(NX, 4, ROWS, EXPERTS, COLS),
+        dw,
     )
     hidden_grad = hidden.reshape(NY, NX, 2, NC, ROWS, TOK).transpose(5, 1, 2, 0, 3, 4).reshape(TOK, -1)
     return layer_out, hidden_grad, weight_grad.transpose(1, 0, 2)

time: 451 us -> 336 us (0.75)
  blocking collectives: 79.8 us -> 0 us
  Pallas kernels: 357 us -> 319 us
    unnamed x1 -> x0, blocking collectives: 79.8 us -> none
    pallas_call x1, Pallas kernels: 95.6 us -> 52.5 us  [body(): pl.pallas_call(compute_kernel, grid_spec=pltpu.PrefetchScalarGridSpec(num...]
    pallas_call x1, Pallas kernels: 131 us -> 135 us  [body(): pl.pallas_call(gather_kernel, out_shape=(shape((NX, EXPERTS, span, COLS),...]
where the time goes in v2:
time: 336 us; the launch traced here: 334 us
  Pallas kernels  319 us (95%)
  local copies, waits for them, and re-layouts  13.2 us (4%)
    pallas_call x1, Pallas kernels, body(): pl.pallas_call(gather_kernel, out_shape=(shape((NX, EXPERTS, span, COLS),...  135 us
    pallas_call x1, Pallas kernels, body(): pl.pallas_call(scatter_kernel, out_shape=(shape((TOK, 4096), bf16), shape...  131 us
    pallas_call x1, Pallas kernels, body(): pl.pallas_call(compute_kernel, grid_spec=pltpu.PrefetchScalarGridSpec(num...  52.5 us

profile of v2, /device:TPU:32, one launch (start us, length us, event | category | flops | bytes accessed | tf_op | source)
XLA Modules:
  0.0 334.2 jit_solution(5584129764893665694)
XLA Ops:
  0.6 0.7 pad.4
  1.3 0.6 broadcast_in_dim.44.pick
  1.9 0.9 reshape.48
  2.8 0.2 copy.30
  3.0 0.1 eq.28
  3.1 0.8 select_reduce_fusion
  4.0 0.1 broadcast_in_dim.51
  4.0 0.1 broadcast_in_dim.52
  4.2 0.1 broadcast_in_dim.48
  4.3 0.1 broadcast_in_dim.49
  4.4 1.2 copy.25
  5.6 0.1 reshape.45
  5.7 0.3 copy.26
  6.0 0.8 copy.27.h
  6.8 135.4 %gather.1 = (bf16[4,64,48,256]{3,2,1,0:T(8,128)(2,1)}, bf16[8,2,4,192,256]{4,3,2,1,0:T(8,128)(2,1)}, bf16[8,2,4,256,256]{4,3,2,1,0:T(8,128)(2,1)}, s32[8,2,4,8,128]{4,3,2,1,0:T(8,128)}) custom-call(bf16[12,64,1024]{2,1,0:T(8,128)(2,1)} %bitcast.36, bf16[4,192,256]{2,1,0:T(8,128)(2,1)} %copy.27.h, bf16[256,4096]{1,0:T(8,128)(2,1)} %g.1, ...), custom_call_target="tpu_custom_call" | custom-call | tf_op jit(solution)/shard_map/gather/pallas_call | solution.py:437
  142.2 1.0 slice.12
  143.2 0.1 eq.27
  143.3 0.5 select_n.21.slots
  143.8 52.5 %compute.1 = (bf16[64,256,256]{2,1,0:T(8,128)(2,1)}, bf16[64,192,256]{2,1,0:T(8,128)(2,1)}, bf16[4,64,48,256]{3,2,1,0:T(8,128)(2,1)}) custom-call(s32[128]{0:T(128)} %select_n.21.slots, bf16[4,64,48,256]{3,2,1,0:T(8,128)(2,1)} %get-tuple-element.14.w, bf16[64,192,256]{2,1,0:T(8,128)(2,1)} %bitcast.33, bf16[64,256,256]{2,1,0:T(8,128)(2,1)} %bitcast.31), custom_call_target="tpu_custom_call" | custom-call | tf_op jit(solution)/shard_map/compute/pallas_call | solution.py:469
  196.3 131.0 %scatter.1 = (bf16[256,4096]{1,0:T(8,128)(2,1)}, bf16[4,192,256]{2,1,0:T(8,128)(2,1)}, bf16[12,64,1024]{2,1,0:T(8,128)(2,1)}) custom-call(bf16[8,2,4,256,256]{4,3,2,1,0:T(8,128)(2,1)} %bitcast.32, bf16[8,2,4,192,256]{4,3,2,1,0:T(8,128)(2,1)} %bitcast.34, bf16[4,64,48,256]{3,2,1,0:T(8,128)(2,1)} %get-tuple-element.19.dw), custom_call_target="tpu_custom_call" | custom-call | tf_op jit(solution)/shard_map/scatter/pallas_call | solution.py:489
  327.4 0.0 copy-start
  327.4 1.4 copy.31
  328.8 0.1 copy.32
  328.9 0.1 reshape.54
  329.0 0.9 copy.33
  329.9 3.1 copy.38
  333.1 0.0 copy-done
  333.1 1.1 copy.39
  (3 shorter events, 0.0 us)
Async XLA Ops:
  327.4 5.7 %copy-start = (bf16[12,64,1024]{2,1,0:T(8,128)(2,1)S(1)}, bf16[12,64,1024]{2,1,0:T(8,128)(2,1)}, u32[]{:S(2)}) copy-start(bf16[12,64,1024]{2,1,0:T(8,128)(2,1)} %get-tuple-element.22) | copy-start | bytes 4718596

commit v3 on v2

--- a/solution.py
+++ b/solution.py
@@ -11,12 +11,18 @@
 BLOCK = 128
 NX, NY, NZ, NC = 4, 4, 8, 2
 ROWS = 12
+SPAN = 4 * ROWS
 GROUP = 192
 COLS = 256
 TOK = 256
 EXPERTS = 64
 VMEM_LIMIT = 60 * 2**20
 OFFSETS = [(dz, dc) for dz in (0, 1, -1, 2, -2, 3, -3, 4) for dc in (0, 1)]
+
+
+WINDOW = 6
+HSTEPS = (6, 9, 12, 15)
+H_BACK = (2, 6, 10, 13)
 
 
 def coords():
@@ -136,7 +142,7 @@
 
     w_state = {}
     bf16 = jnp.bfloat16
-    span = ROWS * 4
+    span = SPAN
 
     def w_step(s):
         if s == 0:
@@ -192,18 +198,21 @@
         g3.append(cp.start(above, above, down_y, gg.at[zs, cs, yof(2), half:TOK]))
 
     steps = len(OFFSETS)
-    for k in range(steps):
+    for k in range(WINDOW):
         g_start(k)
+    h_step(0)
     g_first(0)
-    h_step(0)
     g_first(1)
-    w_step(0)
     for k in range(2, steps):
+        if k - 2 + WINDOW < steps:
+            g_start(k - 2 + WINDOW)
         g_first(k)
+        if k == 3:
+            w_step(0)
         g_second(k - 2)
-        if k in (4, 7, 10, 13):
-            h_step((k - 1) // 3)
-        if k == 8:
+        if k in HSTEPS:
+            h_step(HSTEPS.index(k) + 1)
+        if k == 12:
             w_step(1)
     g_second(steps - 2)
     g_second(steps - 1)
@@ -213,15 +222,14 @@
     cp.drain()
 
 
-def compute_kernel(slots, w, h, g, lo, hgrad, dw, acc):
+def compute_kernel(slots, h, g, dw, acc):
     step = pl.program_id(0)
-    span = ROWS * 4
 
     @pl.when(step == 0)
     def _():
         def clear(e, carry):
             for j in range(NX):
-                acc[j, e] = jnp.zeros((span, COLS), jnp.float32)
+                acc[j, e] = jnp.zeros((SPAN, COLS), jnp.float32)
             return carry
 
         lax.fori_loop(0, EXPERTS, clear, 0)
@@ -229,19 +237,10 @@
     for n in range(h.shape[0]):
         for b in range(TOK // BLOCK):
             slot = slots[(step * h.shape[0] + n) * (TOK // BLOCK) + b]
-            weight = jnp.concatenate([w[j, slot] for j in range(NX)], axis=0)
             tokens = slice(b * BLOCK, (b + 1) * BLOCK)
-            hid = h[n, :, tokens]
-            cot = g[n, tokens, :]
-            lo[n, tokens, :] = lax.dot_general(
-                hid, weight, (((0,), (0,)), ((), ())), preferred_element_type=jnp.float32
-            ).astype(jnp.bfloat16)
-            hgrad[n, :, tokens] = lax.dot_general(
-                weight, cot, (((1,), (1,)), ((), ())), preferred_element_type=jnp.float32
-            ).astype(jnp.bfloat16)
-            outer = jnp.dot(hid, cot, preferred_element_type=jnp.float32)
+            outer = jnp.dot(h[n, :, tokens], g[n, tokens, :], preferred_element_type=jnp.float32)
             for j in range(NX):
-                acc[j, slot] += outer[j * span : (j + 1) * span]
+                acc[j, slot] += outer[j * SPAN : (j + 1) * SPAN]
 
     @pl.when(step == pl.num_programs(0) - 1)
     def _():
@@ -277,9 +276,8 @@
     lax.fori_loop(0, total, one, 0)
 
 
-def scatter_kernel(lo, hp, dw, out, hout, wout, lo_half_up, lo_half_dn, lo_up, lo_dn, sib, hp_up, hp_dn, dw_half_up, dw_half_dn, dw_up, dw_dn, wide, turned, send, recv):
+def scatter_kernel(slots, w, h, g, dw, out, hout, wout, hv, gv, lo_half_up, lo_half_dn, lo_up, lo_dn, sib, hp_up, hp_dn, dw_half_up, dw_half_dn, dw_up, dw_dn, wide, turned, send, recv):
     x, y, z, c = coords()
-    greet(x, y, z, c)
     cp = Copies(send, recv)
     zof = lambda d: (z + d + NZ) % NZ
     yof = lambda d: (y + d + NY) % NY
@@ -291,23 +289,72 @@
     up_x, down_x = device(xof(1), y, z, c), device(xof(-1), y, z, c)
     sibling = device(x, y, z, (c + 1) % 2)
     half = TOK // 2
+    low, high = slice(0, EXPERTS // 2), slice(EXPERTS // 2, EXPERTS)
     order = list(reversed(OFFSETS))
-
-    sib_in = {}
-    for d in (4, 3, -3, 2, -2, 1, -1, 0):
-        zz = zof(d)
-        sib_in[d] = cp.start(hp.at[zz, (c + 1) % 2], sib.at[zz], sibling, sib.at[zz])
-    a_in = []
-    for k, (dz, dc) in enumerate(order):
-        zs, cs = zof(dz), (c + dc) % 2
+    places = [(zof(dz), (c + dc) % 2) for dz, dc in order]
+
+    loads = [(cp.local(h.at[zs, cs], hv.at[zs, cs]), cp.local(g.at[zs, cs], gv.at[zs, cs])) for zs, cs in places]
+    greet(x, y, z, c)
+    d_in = (
+        cp.start(dw.at[xof(2), low], dw_half_up, up_x, dw_half_up),
+        cp.start(dw.at[xof(2), high], dw_half_dn, down_x, dw_half_dn),
+    )
+
+    def products(k):
+        zs, cs = places[k]
+        for copy in loads[k]:
+            copy.wait()
+
+        def one(i, carry):
+            results = []
+            for b in range(TOK // BLOCK):
+                slot = slots[((zs * NC + cs) * NY + i) * (TOK // BLOCK) + b]
+                weight = jnp.concatenate([w[j, slot] for j in range(NX)], axis=0)
+                tokens = slice(b * BLOCK, (b + 1) * BLOCK)
+                hid = hv[zs, cs, i, :, tokens]
+                cot = gv[zs, cs, i, tokens, :]
+                lo = lax.dot_general(hid, weight, (((0,), (0,)), ((), ())), preferred_element_type=jnp.float32)
+                hg = lax.dot_general(weight, cot, (((1,), (1,)), ((), ())), preferred_element_type=jnp.float32)
+                results.append((tokens, lo, hg))
+            for tokens, lo, hg in results:
+                gv[zs, cs, i, tokens, :] = lo.astype(jnp.bfloat16)
+                hv[zs, cs, i, :, tokens] = hg.astype(jnp.bfloat16)
+            return carry
+
+        lax.fori_loop(0, NY, one, 0)
+
+    sib_in, a_in, b_in, o_in = {}, [], [], []
+
+    def lo_first(k):
+        zs, cs = places[k]
         a_in.append((
-            cp.start(lo.at[zs, cs, yof(2), 0:half], lo_half_up.at[k], up_y, lo_half_up.at[k]),
-            cp.start(lo.at[zs, cs, yof(2), half:TOK], lo_half_dn.at[k], down_y, lo_half_dn.at[k]),
+            cp.start(gv.at[zs, cs, yof(2), 0:half], lo_half_up.at[k], up_y, lo_half_up.at[k]),
+            cp.start(gv.at[zs, cs, yof(2), half:TOK], lo_half_dn.at[k], down_y, lo_half_dn.at[k]),
         ))
-    d_in = (
-        cp.start(dw.at[xof(2), 0 : EXPERTS // 2], dw_half_up, up_x, dw_half_up),
-        cp.start(dw.at[xof(2), EXPERTS // 2 : EXPERTS], dw_half_dn, down_x, dw_half_dn),
-    )
+        dz, dc = order[k]
+        if dc:
+            sib_in[dz] = cp.start(hv.at[zs, cs], sib.at[zs], sibling, sib.at[zs])
+
+    def lo_second(k):
+        zs, cs = places[k]
+        a_in[k][0].wait_recv()
+        add_into(gv.at[zs, cs, yof(1), 0:half], lo_half_up.at[k])
+        first = cp.start(gv.at[zs, cs, yof(1)], lo_up.at[k], up_y, lo_up.at[k])
+        a_in[k][1].wait_recv()
+        add_into(gv.at[zs, cs, yof(-1), half:TOK], lo_half_dn.at[k])
+        b_in.append((first, cp.start(gv.at[zs, cs, yof(-1)], lo_dn.at[k], down_y, lo_dn.at[k])))
+
+    def lo_third(k):
+        dz, dc = order[k]
+        zs, cs = places[k]
+        for copy in b_in[k]:
+            copy.wait_recv()
+        add_into(gv.at[zs, cs, y], lo_up.at[k], lo_dn.at[k])
+        mine = out.at[:, quarter(z * 2 + c)]
+        if (dz, dc) == (0, 0):
+            o_in.append(cp.local(gv.at[zs, cs, y], mine))
+        else:
+            o_in.append(cp.start(gv.at[zs, cs, y], mine, device(x, y, zs, cs), out.at[:, quarter(zof(-dz) * 2 + cs)]))
 
     h_state = {}
 
@@ -317,68 +364,44 @@
         if s < 4:
             h_state["up"].wait_recv()
             h_state["down"].wait_recv()
+        first, last = slice(0, 2), slice(2, 4)
         if s == 4:
-            add_into(hp.at[zof(4), c], sib.at[zof(4)])
-            h_state["up"] = cp.start(hp.at[zof(4), c, 0:2], hp_up.at[3, 0:2], up_z, hp_up.at[3, 0:2])
-            h_state["down"] = cp.start(hp.at[zof(4), c, 2:4], hp_dn.at[3, 2:4], down_z, hp_dn.at[3, 2:4])
+            add_into(hv.at[zof(4), c], sib.at[zof(4)])
+            h_state["up"] = cp.start(hv.at[zof(4), c, first], hp_up.at[3, first], up_z, hp_up.at[3, first])
+            h_state["down"] = cp.start(hv.at[zof(4), c, last], hp_dn.at[3, last], down_z, hp_dn.at[3, last])
             return
         if s == 3:
-            add_into(hp.at[zof(3), c, 0:2], sib.at[zof(3), 0:2], hp_up.at[3, 0:2])
-            add_into(hp.at[zof(3), c, 2:4], sib.at[zof(3), 2:4])
-            add_into(hp.at[zof(-3), c, 0:2], sib.at[zof(-3), 0:2])
-            add_into(hp.at[zof(-3), c, 2:4], sib.at[zof(-3), 2:4], hp_dn.at[3, 2:4])
+            add_into(hv.at[zof(3), c, first], sib.at[zof(3), first], hp_up.at[3, first])
+            add_into(hv.at[zof(3), c, last], sib.at[zof(3), last])
+            add_into(hv.at[zof(-3), c, first], sib.at[zof(-3), first])
+            add_into(hv.at[zof(-3), c, last], sib.at[zof(-3), last], hp_dn.at[3, last])
         elif s > 0:
-            add_into(hp.at[zof(s), c], sib.at[zof(s)], hp_up.at[s])
-            add_into(hp.at[zof(-s), c], sib.at[zof(-s)], hp_dn.at[s])
+            add_into(hv.at[zof(s), c], sib.at[zof(s)], hp_up.at[s])
+            add_into(hv.at[zof(-s), c], sib.at[zof(-s)], hp_dn.at[s])
         else:
-            add_into(hp.at[z, c], sib.at[z], hp_up.at[0], hp_dn.at[0])
+            add_into(hv.at[z, c], sib.at[z], hp_up.at[0], hp_dn.at[0])
         if s > 0:
-            h_state["up"] = cp.start(hp.at[zof(s), c], hp_up.at[s - 1], up_z, hp_up.at[s - 1])
-            h_state["down"] = cp.start(hp.at[zof(-s), c], hp_dn.at[s - 1], down_z, hp_dn.at[s - 1])
-
-    b_in, o_in = [], []
-
-    def lo_second(k):
-        dz, dc = order[k]
-        zs, cs = zof(dz), (c + dc) % 2
-        a_in[k][0].wait_recv()
-        add_into(lo.at[zs, cs, yof(1), 0:half], lo_half_up.at[k])
-        first = cp.start(lo.at[zs, cs, yof(1)], lo_up.at[k], up_y, lo_up.at[k])
-        a_in[k][1].wait_recv()
-        add_into(lo.at[zs, cs, yof(-1), half:TOK], lo_half_dn.at[k])
-        b_in.append((first, cp.start(lo.at[zs, cs, yof(-1)], lo_dn.at[k], down_y, lo_dn.at[k])))
-
-    def lo_third(k):
-        dz, dc = order[k]
-        zs, cs = zof(dz), (c + dc) % 2
-        for copy in b_in[k]:
-            copy.wait_recv()
-        add_into(lo.at[zs, cs, y], lo_up.at[k], lo_dn.at[k])
-        mine = out.at[:, quarter(z * 2 + c)]
-        if (dz, dc) == (0, 0):
-            o_in.append(cp.local(lo.at[zs, cs, y], mine))
-        else:
-            o_in.append(cp.start(lo.at[zs, cs, y], mine, device(x, y, zs, cs), out.at[:, quarter(zof(-dz) * 2 + cs)]))
+            h_state["up"] = cp.start(hv.at[zof(s), c], hp_up.at[s - 1], up_z, hp_up.at[s - 1])
+            h_state["down"] = cp.start(hv.at[zof(-s), c], hp_dn.at[s - 1], down_z, hp_dn.at[s - 1])
 
     d_state = {}
 
     def d_step(s):
         if s == 0:
             d_in[0].wait_recv()
-            add_into(dw.at[xof(1), 0 : EXPERTS // 2], dw_half_up)
+            add_into(dw.at[xof(1), low], dw_half_up)
             d_state["up"] = cp.start(dw.at[xof(1)], dw_up, up_x, dw_up)
             d_in[1].wait_recv()
-            add_into(dw.at[xof(-1), EXPERTS // 2 : EXPERTS], dw_half_dn)
+            add_into(dw.at[xof(-1), high], dw_half_dn)
             d_state["down"] = cp.start(dw.at[xof(-1)], dw_dn, down_x, dw_dn)
             return
         d_state["up"].wait_recv()
         d_state["down"].wait_recv()
-        span = ROWS * 4
 
         def turn(e, carry):
             value = dw[x, e].astype(jnp.float32) + dw_up[e].astype(jnp.float32) + dw_dn[e].astype(jnp.float32)
             for j in range(COLS // 128):
-                wide[j, pl.ds(e, span, stride=EXPERTS), :] = value[:, j * 128 : (j + 1) * 128]
+                wide[j, pl.ds(e, SPAN, stride=EXPERTS), :] = value[:, j * 128 : (j + 1) * 128]
             return carry
 
         lax.fori_loop(0, EXPERTS, turn, 0)
@@ -389,30 +412,34 @@
                 turned[i // ROWS, i % ROWS, :, j * 128 : (j + 1) * 128] = wide[j, rows, :].astype(jnp.bfloat16)
             return carry
 
-        lax.fori_loop(0, span, narrow, 0)
+        lax.fori_loop(0, SPAN, narrow, 0)
         for dl, dc in ((1, 0), (1, 1), (0, 1)):
             ol, oc = (zl + dl) % 2, (c + dc) % 2
             there = ol * 2 + oc
             o_in.append(cp.start(turned.at[there], wout.at[:, :, quarter(here)], device(x, y, (z // 2) * 2 + ol, oc), wout.at[:, :, quarter(there)]))
         o_in.append(cp.local(turned.at[here], wout.at[:, :, quarter(here)]))
 
-    h_step(4)
     steps = len(order)
     for k in range(steps):
-        lo_second(k)
-        if k >= 2:
-            lo_third(k - 2)
-        if k in (3, 6, 9, 12):
-            h_step(4 - k // 3)
-        if k == 4:
+        products(k)
+        lo_first(k)
+        if k >= 1:
+            lo_second(k - 1)
+        if k >= 3:
+            lo_third(k - 3)
+        if k in H_BACK:
+            h_step(4 - H_BACK.index(k))
+        if k == 7:
             d_step(0)
-        if k == 10:
-            d_step(1)
+    lo_second(steps - 1)
+    lo_third(steps - 3)
+    d_step(1)
+    lo_third(steps - 2)
+    h_step(0)
     for dy in (1, 3, 2):
         oy = yof(dy)
-        o_in.append(cp.start(hp.at[z, c, oy], hout.at[y], device(x, oy, z, c), hout.at[yof(-dy)]))
-    o_in.append(cp.local(hp.at[z, c, y], hout.at[y]))
-    lo_third(steps - 2)
+        o_in.append(cp.start(hv.at[z, c, oy], hout.at[y], device(x, oy, z, c), hout.at[yof(-dy)]))
+    o_in.append(cp.local(hv.at[z, c, y], hout.at[y]))
     lo_third(steps - 1)
     for copy in o_in:
         if copy.is_remote:
@@ -429,7 +456,6 @@
     vmem = pl.BlockSpec(memory_space=pltpu.VMEM)
     x = lax.axis_index("dev") // 16
 
-    span = ROWS * 4
     ht = hidden_rows.reshape(TOK, NX, 2, NY, NC, ROWS).transpose(3, 1, 2, 4, 5, 0).reshape(NY, GROUP, TOK)
     wt = expert_weights.transpose(1, 0, 2)
     pick = jnp.broadcast_to(jnp.pad(block_pick, (0, 126))[None, :], (8, 128))
@@ -437,7 +463,7 @@
     wg, hg, gg, picks = pl.pallas_call(
         gather_kernel,
         out_shape=(
-            shape((NX, EXPERTS, span, COLS), bf16),
+            shape((NX, EXPERTS, SPAN, COLS), bf16),
             shape((NZ, NC, NY, GROUP, TOK), bf16),
             shape((NZ, NC, NY, TOK, COLS), bf16),
             shape((NZ, NC, NY, 8, 128), jnp.int32),
@@ -446,8 +472,8 @@
         out_specs=(anywhere,) * 4,
         scratch_shapes=[
             pltpu.VMEM((4, ROWS, EXPERTS, COLS), bf16),
-            pltpu.VMEM((COLS // 128, span * EXPERTS, 128), jnp.float32),
-            pltpu.VMEM((EXPERTS, span, COLS), bf16),
+            pltpu.VMEM((COLS // 128, SPAN * EXPERTS, 128), jnp.float32),
+            pltpu.VMEM((EXPERTS, SPAN, COLS), bf16),
             pltpu.SemaphoreType.DMA((160,)),
             pltpu.SemaphoreType.DMA((160,)),
         ],
@@ -463,26 +489,21 @@
     slots = jnp.where(chosen == 0, known[:, 0:1], known[:, 1:2]).reshape(-1)
 
     sources = NZ * NC * NY
-    each = 1
+    each = 2
     one = lambda rows: pl.BlockSpec((each, rows, 256), lambda i, s: (i, 0, 0))
-    whole = lambda: pl.BlockSpec((NX, EXPERTS, span, COLS), lambda i, s: (0, 0, 0, 0), pipeline_mode=pl.Buffered(1))
-    lo, hp, dw = pl.pallas_call(
+    dw = pl.pallas_call(
         compute_kernel,
         grid_spec=pltpu.PrefetchScalarGridSpec(
             num_scalar_prefetch=1,
             grid=(sources // each,),
-            in_specs=[whole(), one(GROUP), one(TOK)],
-            out_specs=(one(TOK), one(GROUP), whole()),
-            scratch_shapes=[pltpu.VMEM((NX, EXPERTS, span, COLS), jnp.float32)],
+            in_specs=[one(GROUP), one(TOK)],
+            out_specs=pl.BlockSpec((NX, EXPERTS, SPAN, COLS), lambda i, s: (0, 0, 0, 0), pipeline_mode=pl.Buffered(1)),
+            scratch_shapes=[pltpu.VMEM((NX, EXPERTS, SPAN, COLS), jnp.float32)],
         ),
-        out_shape=(
-            shape((sources, TOK, COLS), bf16),
-            shape((sources, GROUP, TOK), bf16),
-            shape((NX, EXPERTS, span, COLS), bf16),
-        ),
+        out_shape=shape((NX, EXPERTS, SPAN, COLS), bf16),
         compiler_params=pltpu.CompilerParams(vmem_limit_bytes=VMEM_LIMIT),
-        name="compute",
-    )(slots, wg, hg.reshape(sources, GROUP, TOK), gg.reshape(sources, TOK, COLS))
+        name="weight_gradient",
+    )(slots, hg.reshape(sources, GROUP, TOK), gg.reshape(sources, TOK, COLS))
 
     half = TOK // 2
     pieces = len(OFFSETS)
@@ -493,9 +514,11 @@
             shape((NY, GROUP, TOK), bf16),
             shape((ROWS, EXPERTS, 1024), bf16),
         ),
-        in_specs=[vmem] * 3,
+        in_specs=[pl.BlockSpec(memory_space=pltpu.SMEM), vmem, anywhere, anywhere, vmem],
         out_specs=(anywhere,) * 3,
         scratch_shapes=[
+            pltpu.VMEM((NZ, NC, NY, GROUP, TOK), bf16),
+            pltpu.VMEM((NZ, NC, NY, TOK, COLS), bf16),
             pltpu.VMEM((pieces, half, COLS), bf16),
             pltpu.VMEM((pieces, half, COLS), bf16),
             pltpu.VMEM((pieces, TOK, COLS), bf16),
@@ -503,22 +526,18 @@
             pltpu.VMEM((NZ, NY, GROUP, TOK), bf16),
             pltpu.VMEM((4, NY, GROUP, TOK), bf16),
             pltpu.VMEM((4, NY, GROUP, TOK), bf16),
-            pltpu.VMEM((EXPERTS // 2, span, COLS), bf16),
-            pltpu.VMEM((EXPERTS // 2, span, COLS), bf16),
-            pltpu.VMEM((EXPERTS, span, COLS), bf16),
-            pltpu.VMEM((EXPERTS, span, COLS), bf16),
-            pltpu.VMEM((COLS // 128, span * EXPERTS, 128), jnp.float32),
+            pltpu.VMEM((EXPERTS // 2, SPAN, COLS), bf16),
+            pltpu.VMEM((EXPERTS // 2, SPAN, COLS), bf16),
+            pltpu.VMEM((EXPERTS, SPAN, COLS), bf16),
+            pltpu.VMEM((EXPERTS, SPAN, COLS), bf16),
+            pltpu.VMEM((COLS // 128, SPAN * EXPERTS, 128), jnp.float32),
             pltpu.VMEM((4, ROWS, EXPERTS, COLS), bf16),
-            pltpu.SemaphoreType.DMA((128,)),
-            pltpu.SemaphoreType.DMA((128,)),
+            pltpu.SemaphoreType.DMA((160,)),
+            pltpu.SemaphoreType.DMA((160,)),
         ],
         compiler_params=pltpu.CompilerParams(collective_id=1, has_side_effects=True, vmem_limit_bytes=VMEM_LIMIT),
         name="scatter",
-    )(
-        lo.reshape(NZ, NC, NY, TOK, COLS),
-        hp.reshape(NZ, NC, NY, GROUP, TOK),
-        dw,
-    )
+    )(slots, wg, hg, gg, dw)
     hidden_grad = hidden.reshape(NY, NX, 2, NC, ROWS, TOK).transpose(5, 1, 2, 0, 3, 4).reshape(TOK, -1)
     return layer_out, hidden_grad, weight_grad.transpose(1, 0, 2)
 

time: 336 us -> 281 us (0.84)
  Pallas kernels: 319 us -> 264 us
    pallas_call x1, Pallas kernels: 52.5 us -> 27.1 us  [body(): pl.pallas_call(compute_kernel, grid_spec=pltpu.PrefetchScalarGridSpec(num...]
    pallas_call x1, Pallas kernels: 135 us -> 118 us  [body(): pl.pallas_call(gather_kernel, out_shape=(shape((NX, EXPERTS, SPAN, COLS),...]
    pallas_call x1, Pallas kernels: 131 us -> 118 us  [body(): pl.pallas_call(scatter_kernel, out_shape=(shape((TOK, 4096), bf16), shape...]
where the time goes in v3:
time: 281 us; the launch traced here: 278 us
  Pallas kernels  264 us (94%)
  local copies, waits for them, and re-layouts  12.2 us (4%)
    pallas_call x1, Pallas kernels, body(): pl.pallas_call(scatter_kernel, out_shape=(shape((TOK, 4096), bf16), shape...  118 us
    pallas_call x1, Pallas kernels, body(): pl.pallas_call(gather_kernel, out_shape=(shape((NX, EXPERTS, SPAN, COLS),...  118 us
    pallas_call x1, Pallas kernels, body(): pl.pallas_call(compute_kernel, grid_spec=pltpu.PrefetchScalarGridSpec(num...  27.1 us

profile of v3, /device:TPU:32, one launch (start us, length us, event | category | flops | bytes accessed | tf_op | source)
XLA Modules:
  0.0 278.2 jit_solution(3517385326959206456)
XLA Ops:
  0.6 0.7 pad.4
  1.3 0.6 broadcast_in_dim.44.pick
  1.9 0.9 reshape.42
  2.8 0.2 copy.30
  3.0 0.1 eq.28
  3.1 0.8 select_reduce_fusion
  4.0 0.1 broadcast_in_dim.51
  4.0 0.1 broadcast_in_dim.52
  4.2 0.1 broadcast_in_dim.48
  4.3 0.1 broadcast_in_dim.49
  4.4 1.2 copy.25
  5.6 0.1 reshape.39
  5.7 0.3 copy.26
  6.0 0.8 copy.27.h
  6.8 118.3 %gather.1 = (bf16[4,64,48,256]{3,2,1,0:T(8,128)(2,1)}, bf16[8,2,4,192,256]{4,3,2,1,0:T(8,128)(2,1)}, bf16[8,2,4,256,256]{4,3,2,1,0:T(8,128)(2,1)}, s32[8,2,4,8,128]{4,3,2,1,0:T(8,128)}) custom-call(bf16[12,64,1024]{2,1,0:T(8,128)(2,1)} %bitcast.32, bf16[4,192,256]{2,1,0:T(8,128)(2,1)} %copy.27.h, bf16[256,4096]{1,0:T(8,128)(2,1)} %g.1, ...), custom_call_target="tpu_custom_call" | custom-call | tf_op jit(solution)/shard_map/gather/pallas_call | solution.py:463
  125.1 1.0 slice.12
  126.1 0.1 eq.27
  126.3 0.5 select_n.21.slots
  126.8 27.1 %weight_gradient.1.dw = bf16[4,64,48,256]{3,2,1,0:T(8,128)(2,1)} custom-call(s32[128]{0:T(128)} %select_n.21.slots, bf16[64,192,256]{2,1,0:T(8,128)(2,1)} %bitcast.30, bf16[64,256,256]{2,1,0:T(8,128)(2,1)} %bitcast.29), custom_call_target="tpu_custom_call" | custom-call | tf_op jit(solution)/shard_map/weight_gradient/pallas_call | solution.py:494
  153.9 118.4 %scatter.1 = (bf16[256,4096]{1,0:T(8,128)(2,1)}, bf16[4,192,256]{2,1,0:T(8,128)(2,1)}, bf16[12,64,1024]{2,1,0:T(8,128)(2,1)}) custom-call(s32[128]{0:T(128)} %select_n.21.slots, bf16[4,64,48,256]{3,2,1,0:T(8,128)(2,1)} %get-tuple-element.11.w, bf16[8,2,4,192,256]{4,3,2,1,0:T(8,128)(2,1)} %get-tuple-element.12.h, ...), custom_call_target="tpu_custom_call" | custom-call | tf_op jit(solution)/shard_map/scatter/pallas_call | solution.py:510
  272.3 0.0 copy-start
  272.3 1.5 copy.31
  273.8 0.1 copy.32
  273.9 0.1 reshape.46
  274.0 0.9 copy.33
  274.9 0.0 copy-done
  274.9 0.0 copy-start.1
  274.9 1.3 copy.38
  276.2 0.8 copy-done.1
  277.1 1.1 copy.39
  (3 shorter events, 0.0 us)
Async XLA Ops:
  272.3 2.6 copy-start
  274.9 2.2 copy-start.1

commit v4 on v3

--- a/solution.py
+++ b/solution.py
@@ -21,7 +21,8 @@
 
 
 WINDOW = 6
-HSTEPS = (6, 9, 12, 15)
+HSTEPS = (5, 8, 11)
+WEIGH = (0, 0, 0, 0, 1, 2, 3, 4, 5, 6, 7, 8, 9, 10, 11, 12)
 H_BACK = (2, 6, 10, 13)
 
 
@@ -73,7 +74,7 @@
     return pl.ds(pl.multiple_of(q * COLS, COLS), COLS)
 
 
-def gather_kernel(w, h, g, pick, wg, hg, gg, picks, landed, wide, turned, send, recv):
+def gather_kernel(chain, w, h, g, pick, wg, hg_out, gg_out, picks_out, dw_out, hg, gg, picks, sums, dw, landed, wide, turned, send, recv):
     x, y, z, c = coords()
     greet(x, y, z, c)
     cp = Copies(send, recv)
@@ -119,7 +120,7 @@
     sibling = device(x, y, z, (c + 1) % 2)
 
     h_state = []
-    h_sib = []
+    h_sib = {}
 
     def h_send(pairs, target, back):
         for ref, at, land in pairs:
@@ -137,8 +138,10 @@
             low, high = slice(0, 2), slice(2, 4)
             h_send([(hg, (behind, c, low), (zof(-4), c, low)), (picks, (behind, c, low), (zof(-4), c, low))], up_z, h_state)
             h_send([(hg, (ahead, c, high), (zof(4), c, high)), (picks, (ahead, c, high), (zof(4), c, high))], down_z, h_state)
-        for zz in [behind] if s in (0, 4) else [behind, ahead]:
-            h_send([(r, (zz, c), (zz, (c + 1) % 2)) for r in (hg, picks)], sibling, h_sib)
+        for d in (-s,) if s in (0, 4) else (-s, s):
+            zz = zof(d)
+            h_sib[d] = []
+            h_send([(r, (zz, c), (zz, (c + 1) % 2)) for r in (hg, picks)], sibling, h_sib[d])
 
     w_state = {}
     bf16 = jnp.bfloat16
@@ -194,8 +197,41 @@
             wait(copy)
         below = gg.at[zs, cs, yof(-1), 0:half]
         above = gg.at[zs, cs, yof(1), half:TOK]
-        g3.append(cp.start(below, below, up_y, gg.at[zs, cs, yof(-2), 0:half]))
-        g3.append(cp.start(above, above, down_y, gg.at[zs, cs, yof(2), half:TOK]))
+        g3.append((
+            cp.start(below, below, up_y, gg.at[zs, cs, yof(-2), 0:half]),
+            cp.start(above, above, down_y, gg.at[zs, cs, yof(2), half:TOK]),
+        ))
+
+    outward = []
+
+    def weigh(k):
+        dz, dc = OFFSETS[k]
+        zs, cs = zof(-dz), (c + dc) % 2
+        for copy in list(g3[k]) + (h_sib[-dz] if dc else []):
+            wait(copy)
+        outward.append(cp.local(hg.at[zs, cs], hg_out.at[zs, cs]))
+        outward.append(cp.local(gg.at[zs, cs], gg_out.at[zs, cs]))
+
+        def one(i, carry):
+            at = ((zs * NC + cs) * NY + i) * 2
+            which = picks[zs, cs, i]
+            mask = jnp.concatenate([which[0:1], which[1:2]], axis=1).astype(jnp.float32).astype(bf16)
+            hid, cot = hg[zs, cs, i], gg[zs, cs, i]
+            second = hid * mask
+            first = hid - second
+            total = [
+                sums[chain[at + n]] + jnp.dot(part, cot, preferred_element_type=jnp.float32)
+                for n, part in enumerate((first, second))
+            ]
+            for n in range(2):
+                sums[at + n] = total[n]
+            return carry
+
+        lax.fori_loop(0, NY, one, 0)
+
+    def clear(i, carry):
+        sums[i] = jnp.zeros((GROUP, COLS), jnp.float32)
+        return carry
 
     steps = len(OFFSETS)
     for k in range(WINDOW):
@@ -203,6 +239,8 @@
     h_step(0)
     g_first(0)
     g_first(1)
+    lax.fori_loop(0, 2 * NZ * NC * NY + 1, clear, 0)
+    weighed = 0
     for k in range(2, steps):
         if k - 2 + WINDOW < steps:
             g_start(k - 2 + WINDOW)
@@ -214,42 +252,31 @@
             h_step(HSTEPS.index(k) + 1)
         if k == 12:
             w_step(1)
+        while weighed < WEIGH[k]:
+            weigh(weighed)
+            weighed += 1
     g_second(steps - 2)
     g_second(steps - 1)
+    while weighed < steps - 2:
+        weigh(weighed)
+        weighed += 1
+    h_step(4)
+    for k in range(steps - 2, steps):
+        weigh(k)
+    outward.append(cp.local(picks, picks_out))
+
+    def settle(e, carry):
+        value = sums[chain[2 * NZ * NC * NY + e]]
+        for j in range(NX):
+            dw[j, e] = value[j * SPAN : (j + 1) * SPAN].astype(bf16)
+        return carry
+
+    lax.fori_loop(0, EXPERTS, settle, 0)
+    outward.append(cp.local(dw, dw_out))
     w_step(2)
-    for copy in g3 + h_sib:
+    for copy in outward:
         wait(copy)
     cp.drain()
-
-
-def compute_kernel(slots, h, g, dw, acc):
-    step = pl.program_id(0)
-
-    @pl.when(step == 0)
-    def _():
-        def clear(e, carry):
-            for j in range(NX):
-                acc[j, e] = jnp.zeros((SPAN, COLS), jnp.float32)
-            return carry
-
-        lax.fori_loop(0, EXPERTS, clear, 0)
-
-    for n in range(h.shape[0]):
-        for b in range(TOK // BLOCK):
-            slot = slots[(step * h.shape[0] + n) * (TOK // BLOCK) + b]
-            tokens = slice(b * BLOCK, (b + 1) * BLOCK)
-            outer = jnp.dot(h[n, :, tokens], g[n, tokens, :], preferred_element_type=jnp.float32)
-            for j in range(NX):
-                acc[j, slot] += outer[j * SPAN : (j + 1) * SPAN]
-
-    @pl.when(step == pl.num_programs(0) - 1)
-    def _():
-        def empty(e, carry):
-            for j in range(NX):
-                dw[j, e] = acc[j, e].astype(jnp.bfloat16)
-            return carry
-
-        lax.fori_loop(0, EXPERTS, empty, 0)
 
 
 def add_into(dst, *others):
@@ -276,7 +303,7 @@
     lax.fori_loop(0, total, one, 0)
 
 
-def scatter_kernel(slots, w, h, g, dw, out, hout, wout, hv, gv, lo_half_up, lo_half_dn, lo_up, lo_dn, sib, hp_up, hp_dn, dw_half_up, dw_half_dn, dw_up, dw_dn, wide, turned, send, recv):
+def scatter_kernel(slots, w_in, h, g, dw_in, out, hout, wout, w, dw, hv, gv, lo_half_up, lo_half_dn, lo_up, lo_dn, sib, hp_up, hp_dn, dw_half_up, dw_half_dn, dw_up, dw_dn, wide, turned, send, recv):
     x, y, z, c = coords()
     cp = Copies(send, recv)
     zof = lambda d: (z + d + NZ) % NZ
@@ -293,8 +320,11 @@
     order = list(reversed(OFFSETS))
     places = [(zof(dz), (c + dc) % 2) for dz, dc in order]
 
+    w_load = cp.local(w_in, w)
+    dw_loads = [cp.local(dw_in.at[xof(d)], dw.at[xof(d)]) for d in (2, 1, -1, 0)]
     loads = [(cp.local(h.at[zs, cs], hv.at[zs, cs]), cp.local(g.at[zs, cs], gv.at[zs, cs])) for zs, cs in places]
     greet(x, y, z, c)
+    dw_loads[0].wait()
     d_in = (
         cp.start(dw.at[xof(2), low], dw_half_up, up_x, dw_half_up),
         cp.start(dw.at[xof(2), high], dw_half_dn, down_x, dw_half_dn),
@@ -388,6 +418,8 @@
 
     def d_step(s):
         if s == 0:
+            for copy in dw_loads[1:]:
+                copy.wait()
             d_in[0].wait_recv()
             add_into(dw.at[xof(1), low], dw_half_up)
             d_state["up"] = cp.start(dw.at[xof(1)], dw_up, up_x, dw_up)
@@ -420,6 +452,7 @@
         o_in.append(cp.local(turned.at[here], wout.at[:, :, quarter(here)]))
 
     steps = len(order)
+    w_load.wait()
     for k in range(steps):
         products(k)
         lo_first(k)
@@ -453,57 +486,58 @@
     bf16 = jnp.bfloat16
     shape = jax.ShapeDtypeStruct
     anywhere = pl.BlockSpec(memory_space=pl.ANY)
-    vmem = pl.BlockSpec(memory_space=pltpu.VMEM)
-    x = lax.axis_index("dev") // 16
-
     ht = hidden_rows.reshape(TOK, NX, 2, NY, NC, ROWS).transpose(3, 1, 2, 4, 5, 0).reshape(NY, GROUP, TOK)
     wt = expert_weights.transpose(1, 0, 2)
-    pick = jnp.broadcast_to(jnp.pad(block_pick, (0, 126))[None, :], (8, 128))
-
-    wg, hg, gg, picks = pl.pallas_call(
+    pick = jnp.broadcast_to(jnp.pad(block_pick, (0, 6))[:, None], (8, 128))
+
+    x, y, z, c = coords()
+    needs = need_lists.reshape(4, NX, 2, NY, NC, 2)
+    needs = lax.dynamic_index_in_dim(needs, x, 1, keepdims=False).transpose(0, 1, 3, 2, 4).reshape(-1)
+    ids = jnp.arange(EXPERTS, dtype=jnp.int32)
+    known = jnp.sum(jnp.where(needs[:, None] == ids, owner_slot[None, :], 0), axis=1)
+    count = known.shape[0]
+    place = jnp.arange(count, dtype=jnp.int32)
+    far = (z - place // (NC * NY * 2) + NZ) % NZ
+    turn = jnp.where(far == 0, 0, jnp.where(far <= NZ // 2, 2 * far - 1, 2 * (NZ - far)))
+    rank = (turn * NC + (place // (NY * 2) % NC + c) % NC) * (NY * 2) + place % (NY * 2)
+    key = rank * count + place
+    before = jnp.max(jnp.where((known[:, None] == known[None, :]) & (key[None, :] < key[:, None]), key[None, :], -1), axis=1)
+    final = jnp.max(jnp.where(ids[:, None] == known[None, :], key[None, :], -1), axis=1)
+    chain = jnp.concatenate([before, final])
+    chain = jnp.where(chain < 0, count, chain % count)
+
+    smem = pl.BlockSpec(memory_space=pltpu.SMEM)
+    gathered = (
+        shape((NX, EXPERTS, SPAN, COLS), bf16),
+        shape((NZ, NC, NY, GROUP, TOK), bf16),
+        shape((NZ, NC, NY, TOK, COLS), bf16),
+        shape((NZ, NC, NY, 8, 128), jnp.int32),
+        shape((NX, EXPERTS, SPAN, COLS), bf16),
+    )
+    wg, hg, gg, picks, dw = pl.pallas_call(
         gather_kernel,
-        out_shape=(
-            shape((NX, EXPERTS, SPAN, COLS), bf16),
-            shape((NZ, NC, NY, GROUP, TOK), bf16),
-            shape((NZ, NC, NY, TOK, COLS), bf16),
-            shape((NZ, NC, NY, 8, 128), jnp.int32),
-        ),
-        in_specs=[anywhere] * 4,
-        out_specs=(anywhere,) * 4,
+        out_shape=gathered,
+        in_specs=[smem] + [anywhere] * 4,
+        out_specs=(anywhere,) * 5,
         scratch_shapes=[
+            pltpu.VMEM((NZ, NC, NY, GROUP, TOK), bf16),
+            pltpu.VMEM((NZ, NC, NY, TOK, COLS), bf16),
+            pltpu.VMEM((NZ, NC, NY, 8, 128), jnp.int32),
+            pltpu.VMEM((count + 1, GROUP, COLS), jnp.float32),
+            pltpu.VMEM((NX, EXPERTS, SPAN, COLS), bf16),
             pltpu.VMEM((4, ROWS, EXPERTS, COLS), bf16),
             pltpu.VMEM((COLS // 128, SPAN * EXPERTS, 128), jnp.float32),
             pltpu.VMEM((EXPERTS, SPAN, COLS), bf16),
-            pltpu.SemaphoreType.DMA((160,)),
-            pltpu.SemaphoreType.DMA((160,)),
+            pltpu.SemaphoreType.DMA((200,)),
+            pltpu.SemaphoreType.DMA((200,)),
         ],
         compiler_params=pltpu.CompilerParams(collective_id=0, has_side_effects=True, vmem_limit_bytes=VMEM_LIMIT),
         name="gather",
-    )(wt, ht, out_grad, pick)
-
-    needs = need_lists.reshape(4, NX, 2, NY, NC, 2)
-    needs = lax.dynamic_index_in_dim(needs, x, 1, keepdims=False).transpose(0, 1, 3, 2, 4).reshape(-1, 2)
-    ids = jnp.arange(EXPERTS, dtype=jnp.int32)
-    known = jnp.sum(jnp.where(needs[:, :, None] == ids, owner_slot[None, None, :], 0), axis=2)
-    chosen = picks.reshape(-1, 8, 128)[:, 0, 0:2]
+    )(chain, wt, ht, out_grad, pick)
+
+    known = known.reshape(-1, 2)
+    chosen = picks.reshape(-1, 8, 128)[:, 0:2, 0]
     slots = jnp.where(chosen == 0, known[:, 0:1], known[:, 1:2]).reshape(-1)
-
-    sources = NZ * NC * NY
-    each = 2
-    one = lambda rows: pl.BlockSpec((each, rows, 256), lambda i, s: (i, 0, 0))
-    dw = pl.pallas_call(
-        compute_kernel,
-        grid_spec=pltpu.PrefetchScalarGridSpec(
-            num_scalar_prefetch=1,
-            grid=(sources // each,),
-            in_specs=[one(GROUP), one(TOK)],
-            out_specs=pl.BlockSpec((NX, EXPERTS, SPAN, COLS), lambda i, s: (0, 0, 0, 0), pipeline_mode=pl.Buffered(1)),
-            scratch_shapes=[pltpu.VMEM((NX, EXPERTS, SPAN, COLS), jnp.float32)],
-        ),
-        out_shape=shape((NX, EXPERTS, SPAN, COLS), bf16),
-        compiler_params=pltpu.CompilerParams(vmem_limit_bytes=VMEM_LIMIT),
-        name="weight_gradient",
-    )(slots, hg.reshape(sources, GROUP, TOK), gg.reshape(sources, TOK, COLS))
 
     half = TOK // 2
     pieces = len(OFFSETS)
@@ -514,9 +548,11 @@
             shape((NY, GROUP, TOK), bf16),
             shape((ROWS, EXPERTS, 1024), bf16),
         ),
-        in_specs=[pl.BlockSpec(memory_space=pltpu.SMEM), vmem, anywhere, anywhere, vmem],
+        in_specs=[smem] + [anywhere] * 4,
         out_specs=(anywhere,) * 3,
         scratch_shapes=[
+            pltpu.VMEM((NX, EXPERTS, SPAN, COLS), bf16),
+            pltpu.VMEM((NX, EXPERTS, SPAN, COLS), bf16),
             pltpu.VMEM((NZ, NC, NY, GROUP, TOK), bf16),
             pltpu.VMEM((NZ, NC, NY, TOK, COLS), bf16),
             pltpu.VMEM((pieces, half, COLS), bf16),

time: 281 us -> 252 us (0.90)
  Pallas kernels: 264 us -> 233 us
    pallas_call x2 -> x1, Pallas kernels: 145 us -> 119 us  [body(): pl.pallas_call(gather_kernel, out_shape=gathered, in_specs=[smem] + [anyw...]
    pallas_call x1, Pallas kernels: 118 us -> 114 us  [body(): pl.pallas_call(scatter_kernel, out_shape=(shape((TOK, 4096), bf16), shape...]
    unnamed x8 -> x9, local copies, waits for them, and re-layouts: 5.4 us -> 5.89 us
where the time goes in v4:
time: 252 us; the launch traced here: 249 us
  Pallas kernels  233 us (92%)
  local copies, waits for them, and re-layouts  13.2 us (5%)
    pallas_call x1, Pallas kernels, body(): pl.pallas_call(gather_kernel, out_shape=gathered, in_specs=[smem] + [anyw...  119 us
    pallas_call x1, Pallas kernels, body(): pl.pallas_call(scatter_kernel, out_shape=(shape((TOK, 4096), bf16), shape...  114 us
    unnamed x9, local copies, waits for them, and re-layouts  5.89 us

profile of v4, /device:TPU:32, one launch (start us, length us, event | category | flops | bytes accessed | tf_op | source)
XLA Modules:
  0.0 249.4 jit_solution(15288891456847485460)
XLA Ops:
  0.7 0.7 pad.4
  1.4 0.7 broadcast_in_dim.86.pick
  2.0 0.9 reshape.196
  2.9 0.3 copy.24
  3.2 0.1 eq.71
  3.4 0.7 select_reduce_fusion.2
  4.1 0.1 select_reduce_fusion.1
  4.3 0.2 select_reduce_fusion
  4.4 0.6 fusion.chain
  5.0 0.1 reshape.200
  5.2 0.2 slice_reduce_fusion
  5.3 0.1 broadcast_in_dim.91
  5.4 0.2 broadcast_in_dim.92
  5.6 0.1 broadcast_in_dim.88
  5.6 0.1 broadcast_in_dim.89
  5.8 1.2 copy.25
  7.0 0.1 reshape.197
  7.1 0.3 copy.26
  7.4 0.8 copy.27.h
  8.2 118.7 %gather.1 = (bf16[4,64,48,256]{3,2,1,0:T(8,128)(2,1)}, bf16[8,2,4,192,256]{4,3,2,1,0:T(8,128)(2,1)}, bf16[8,2,4,256,256]{4,3,2,1,0:T(8,128)(2,1)}, s32[8,2,4,8,128]{4,3,2,1,0:T(8,128)}, bf16[4,64,48,256]{3,2,1,0:T(8,128)(2,1)}) custom-call(s32[192]{0:T(256)} %fusion.chain, bf16[12,64,1024]{2,1,0:T(8,128)(2,1)} %bitcast.24, bf16[4,192,256]{2,1,0:T(8,128)(2,1)} %copy.27.h, ...), custom_call_target="tpu_custom_call" | custom-call | tf_op jit(solution)/shard_map/gather/pallas_call | solution.py:517
  126.9 1.0 slice.12
  127.9 0.5 copy.33
  128.3 0.1 eq.83
  128.5 0.5 select_n.164.slots
  129.0 114.4 %scatter.1 = (bf16[256,4096]{1,0:T(8,128)(2,1)}, bf16[4,192,256]{2,1,0:T(8,128)(2,1)}, bf16[12,64,1024]{2,1,0:T(8,128)(2,1)}) custom-call(s32[128]{0:T(128)} %select_n.164.slots, bf16[4,64,48,256]{3,2,1,0:T(8,128)(2,1)} %get-tuple-element.12.w_in, bf16[8,2,4,192,256]{4,3,2,1,0:T(8,128)(2,1)} %get-tuple-element.13.h, ...), custom_call_target="tpu_custom_call" | custom-call | tf_op jit(solution)/shard_map/scatter/pallas_call | solution.py:544
  243.5 1.5 copy.29
  244.9 0.1 copy.30
  245.0 0.1 reshape.202
  245.1 0.9 copy.31
  246.0 1.3 copy.36
  247.4 0.8 copy-done.1
  248.2 1.1 copy.37
  (6 shorter events, 0.1 us)
Async XLA Ops:
  243.5 2.6 %copy-start = (bf16[256,4096]{1,0:T(8,128)(2,1)S(1)}, bf16[256,4096]{1,0:T(8,128)(2,1)}, u32[]{:S(2)}) copy-start(bf16[256,4096]{1,0:T(8,128)(2,1)} %get-tuple-element.30) | copy-start | bytes 6291460
  246.0 2.2 copy-start.1

commit v5 on v4

--- a/solution.py
+++ b/solution.py
@@ -24,6 +24,9 @@
 HSTEPS = (5, 8, 11)
 WEIGH = (0, 0, 0, 0, 1, 2, 3, 4, 5, 6, 7, 8, 9, 10, 11, 12)
 H_BACK = (2, 6, 10, 13)
+D_BACK = (4, 12)
+W_PARTS = (0, 2, 3, 4)
+W_STEPS = (6, 14)
 
 
 def coords():
@@ -67,16 +70,24 @@
     others += [((x + dx) % NX, y, z, c) for dx in (1, 3)]
     for other in others:
         pl.semaphore_signal(barrier, inc=1, device_id=device(*other), device_id_type=MESH)
-    pl.semaphore_wait(barrier, len(others))
+    return lambda: pl.semaphore_wait(barrier, len(others))
 
 
 def quarter(q):
     return pl.ds(pl.multiple_of(q * COLS, COLS), COLS)
 
 
-def gather_kernel(chain, w, h, g, pick, wg, hg_out, gg_out, picks_out, dw_out, hg, gg, picks, sums, dw, landed, wide, turned, send, recv):
+def gather_kernel(chain, own, w, h, g, wg, hg_out, gg_out, picks_out, dw_out, hg, gg, picks, sums, dw, landed, wide, turned, pick, send, recv):
     x, y, z, c = coords()
-    greet(x, y, z, c)
+    met = greet(x, y, z, c)
+    pick[...] = jnp.where(lax.broadcasted_iota(jnp.int32, (8, 128), 0) == 0, own[0], own[1])
+
+    def clear(i, carry):
+        sums[i] = jnp.zeros((GROUP, COLS), jnp.float32)
+        return carry
+
+    lax.fori_loop(0, 2 * NZ * NC * NY + 1, clear, 0)
+    met()
     cp = Copies(send, recv)
     zof = lambda d: (z + d + NZ) % NZ
     yof = lambda d: (y + d + NY) % NY
@@ -91,12 +102,14 @@
         h1.append(cp.start(pick, picks.at[z, c, y], device(x, oy, z, c), picks.at[z, c, yof(-dy)]))
     h1.append(cp.local(h.at[y], hg.at[z, c, y]))
     h1.append(cp.local(pick, picks.at[z, c, y]))
-    w1 = []
-    for dl, dc in ((1, 0), (1, 1), (0, 1)):
-        ol, oc = (zl + dl) % 2, (c + dc) % 2
-        there = ol * 2 + oc
-        w1.append(cp.start(w.at[:, :, quarter(there)], landed.at[here], device(x, y, (z // 2) * 2 + ol, oc), landed.at[there]))
-    w1.append(cp.local(w.at[:, :, quarter(here)], landed.at[here]))
+    w1 = [cp.local(w.at[:, :, quarter(here)], landed.at[here])]
+
+    def w_start(part, parts):
+        rows = slice(part * ROWS // parts, (part + 1) * ROWS // parts)
+        for dl, dc in ((1, 0), (1, 1), (0, 1)):
+            ol, oc = (zl + dl) % 2, (c + dc) % 2
+            there = ol * 2 + oc
+            w1.append(cp.start(w.at[rows, :, quarter(there)], landed.at[here, rows], device(x, y, (z // 2) * 2 + ol, oc), landed.at[there, rows]))
 
     g1 = []
 
@@ -229,28 +242,28 @@
 
         lax.fori_loop(0, NY, one, 0)
 
-    def clear(i, carry):
-        sums[i] = jnp.zeros((GROUP, COLS), jnp.float32)
-        return carry
-
     steps = len(OFFSETS)
+    for part in range(W_PARTS.count(0)):
+        w_start(part, len(W_PARTS))
     for k in range(WINDOW):
         g_start(k)
     h_step(0)
     g_first(0)
     g_first(1)
-    lax.fori_loop(0, 2 * NZ * NC * NY + 1, clear, 0)
     weighed = 0
     for k in range(2, steps):
         if k - 2 + WINDOW < steps:
             g_start(k - 2 + WINDOW)
+        for part in range(len(W_PARTS)):
+            if W_PARTS[part] == k:
+                w_start(part, len(W_PARTS))
         g_first(k)
-        if k == 3:
+        if k == W_STEPS[0]:
             w_step(0)
         g_second(k - 2)
         if k in HSTEPS:
             h_step(HSTEPS.index(k) + 1)
-        if k == 12:
+        if k == W_STEPS[1]:
             w_step(1)
         while weighed < WEIGH[k]:
             weigh(weighed)
@@ -323,12 +336,14 @@
     w_load = cp.local(w_in, w)
     dw_loads = [cp.local(dw_in.at[xof(d)], dw.at[xof(d)]) for d in (2, 1, -1, 0)]
     loads = [(cp.local(h.at[zs, cs], hv.at[zs, cs]), cp.local(g.at[zs, cs], gv.at[zs, cs])) for zs, cs in places]
-    greet(x, y, z, c)
-    dw_loads[0].wait()
-    d_in = (
-        cp.start(dw.at[xof(2), low], dw_half_up, up_x, dw_half_up),
-        cp.start(dw.at[xof(2), high], dw_half_dn, down_x, dw_half_dn),
-    )
+    met = greet(x, y, z, c)
+
+    def start_weights():
+        dw_loads[0].wait()
+        return (
+            cp.start(dw.at[xof(2), low], dw_half_up, up_x, dw_half_up),
+            cp.start(dw.at[xof(2), high], dw_half_dn, down_x, dw_half_dn),
+        )
 
     def products(k):
         zs, cs = places[k]
@@ -453,8 +468,12 @@
 
     steps = len(order)
     w_load.wait()
+    products(0)
+    met()
+    d_in = start_weights()
     for k in range(steps):
-        products(k)
+        if k > 0:
+            products(k)
         lo_first(k)
         if k >= 1:
             lo_second(k - 1)
@@ -462,11 +481,12 @@
             lo_third(k - 3)
         if k in H_BACK:
             h_step(4 - H_BACK.index(k))
-        if k == 7:
-            d_step(0)
+        if k in D_BACK:
+            d_step(D_BACK.index(k))
     lo_second(steps - 1)
     lo_third(steps - 3)
-    d_step(1)
+    if len(D_BACK) < 2:
+        d_step(1)
     lo_third(steps - 2)
     h_step(0)
     for dy in (1, 3, 2):
@@ -488,7 +508,6 @@
     anywhere = pl.BlockSpec(memory_space=pl.ANY)
     ht = hidden_rows.reshape(TOK, NX, 2, NY, NC, ROWS).transpose(3, 1, 2, 4, 5, 0).reshape(NY, GROUP, TOK)
     wt = expert_weights.transpose(1, 0, 2)
-    pick = jnp.broadcast_to(jnp.pad(block_pick, (0, 6))[:, None], (8, 128))
 
     x, y, z, c = coords()
     needs = need_lists.reshape(4, NX, 2, NY, NC, 2)
@@ -517,7 +536,7 @@
     wg, hg, gg, picks, dw = pl.pallas_call(
         gather_kernel,
         out_shape=gathered,
-        in_specs=[smem] + [anywhere] * 4,
+        in_specs=[smem] * 2 + [anywhere] * 3,
         out_specs=(anywhere,) * 5,
         scratch_shapes=[
             pltpu.VMEM((NZ, NC, NY, GROUP, TOK), bf16),
@@ -528,12 +547,13 @@
             pltpu.VMEM((4, ROWS, EXPERTS, COLS), bf16),
             pltpu.VMEM((COLS // 128, SPAN * EXPERTS, 128), jnp.float32),
             pltpu.VMEM((EXPERTS, SPAN, COLS), bf16),
+            pltpu.VMEM((8, 128), jnp.int32),
             pltpu.SemaphoreType.DMA((200,)),
             pltpu.SemaphoreType.DMA((200,)),
         ],
         compiler_params=pltpu.CompilerParams(collective_id=0, has_side_effects=True, vmem_limit_bytes=VMEM_LIMIT),
         name="gather",
-    )(chain, wt, ht, out_grad, pick)
+    )(chain, block_pick, wt, ht, out_grad)
 
     known = known.reshape(-1, 2)
     chosen = picks.reshape(-1, 8, 128)[:, 0:2, 0]

time: 252 us -> 250 us (level)
  no operation moved by 1% of the time
where the time goes in v5:
time: 250 us
  Pallas kernels  235 us (94%)
  local copies, waits for them, and re-layouts  11.9 us (5%)
    pallas_call x1, Pallas kernels, body(): pl.pallas_call(gather_kernel, out_shape=gathered, in_specs=[smem] * 2 + [...  119 us
    pallas_call x1, Pallas kernels, body(): pl.pallas_call(scatter_kernel, out_shape=(shape((TOK, 4096), bf16), shape...  115 us
    unnamed x9, local copies, waits for them, and re-layouts  5.89 us

profile of v5, /device:TPU:32, one launch (start us, length us, event | category | flops | bytes accessed | tf_op | source)
XLA Modules:
  0.0 249.5 jit_solution(15708886555712927422)
XLA Ops:
  0.7 0.9 reshape.195
  1.6 0.3 copy.24
  1.9 0.1 eq.71
  2.1 0.7 select_reduce_fusion.2
  2.8 0.1 select_reduce_fusion.1
  2.9 0.2 select_reduce_fusion
  3.1 0.6 fusion.chain
  3.7 0.1 reshape.199
  3.8 0.2 slice_reduce_fusion
  4.0 0.1 broadcast_in_dim.84
  4.1 0.2 broadcast_in_dim.85
  4.2 0.1 broadcast_in_dim.81
  4.3 0.1 broadcast_in_dim.82
  4.5 1.2 copy.25
  5.6 0.1 reshape.196
  5.7 0.3 copy.26
  6.1 0.8 copy.27.h
  6.8 119.4 %gather.1 = (bf16[4,64,48,256]{3,2,1,0:T(8,128)(2,1)}, bf16[8,2,4,192,256]{4,3,2,1,0:T(8,128)(2,1)}, bf16[8,2,4,256,256]{4,3,2,1,0:T(8,128)(2,1)}, s32[8,2,4,8,128]{4,3,2,1,0:T(8,128)}, bf16[4,64,48,256]{3,2,1,0:T(8,128)(2,1)}) custom-call(s32[192]{0:T(256)} %fusion.chain, s32[2]{0:T(128)} %own.1, bf16[12,64,1024]{2,1,0:T(8,128)(2,1)} %bitcast.21, ...), custom_call_target="tpu_custom_call" | custom-call | tf_op jit(solution)/shard_map/gather/pallas_call | solution.py:536
  126.2 1.0 slice.12
  127.2 0.5 copy.33
  127.7 0.1 eq.83
  127.8 0.5 select_n.164.slots
  128.3 115.3 %scatter.1 = (bf16[256,4096]{1,0:T(8,128)(2,1)}, bf16[4,192,256]{2,1,0:T(8,128)(2,1)}, bf16[12,64,1024]{2,1,0:T(8,128)(2,1)}) custom-call(s32[128]{0:T(128)} %select_n.164.slots, bf16[4,64,48,256]{3,2,1,0:T(8,128)(2,1)} %get-tuple-element.12.w_in, bf16[8,2,4,192,256]{4,3,2,1,0:T(8,128)(2,1)} %get-tuple-element.13.h, ...), custom_call_target="tpu_custom_call" | custom-call | tf_op jit(solution)/shard_map/scatter/pallas_call | solution.py:564
  243.6 0.0 copy-start
  243.7 1.5 copy.29
  245.1 0.1 copy.30
  245.2 0.1 reshape.201
  245.3 0.9 copy.31
  246.2 0.0 copy-done
  246.2 1.3 copy.36
  247.5 0.8 copy-done.1
  248.4 1.1 copy.37
  (4 shorter events, 0.0 us)
Async XLA Ops:
  243.6 2.6 %copy-start = (bf16[256,4096]{1,0:T(8,128)(2,1)S(1)}, bf16[256,4096]{1,0:T(8,128)(2,1)}, u32[]{:S(2)}) copy-start(bf16[256,4096]{1,0:T(8,128)(2,1)} %get-tuple-element.30) | copy-start | bytes 6291460
  246.2 2.2 copy-start.1
